TPU v7x, 128 devices: a whole 4x4x4 slice. The times are simulated.
128 devices in a mesh: layer: 8 (over x_lo, z), example: 16 (over x_hi, y, core).
Axes of the slice: x: 4 (x_hi: 2, x_lo: 2; x = x_hi * 2 + x_lo), y: 4, z: 4, core: 2. Of those that a mesh axis runs over, the one named last changes fastest.
Arguments:
- queries: float32 [8, 256, 1024], P('layer', 'example'), may hold values from -0.0625 to 0.0625
- precond: float32 [8, 1024, 1024], P('layer', 'example'), may hold values from -7 to 7.5, as said below
- store: float32 [8, 65536, 1024], P('layer', 'example'), may hold values from -2000 to 2000
Outputs:
- influence: float32 [256, 65536], P('layer', 'example')
Inputs may be any that keep to these rules, and one draw needn't show every extreme that they name: `precond`: each layer's preconditioner is symmetric positive definite, a damped Gram matrix with every eigenvalue at least 0.25.
All inputs are finite; a program needn't handle non-finite values.
Results may differ from a plain program's by a relative error of at most 0.0001.
Values sent between devices are 32-bit elements; how exact they have to be, the bound alone decides.
No kernel may reach another device: no remote copies, remote signals or barrier semaphores. Data moves between devices by JAX's collectives and lax.ppermute only.
A program may use at most 128 MiB of HBM per device.

v0:
```python
import jax
import jax.numpy as jnp
from jax import lax
from jax.sharding import PartitionSpec as P


def shards(queries, precond, store):
    full_matrix = lax.all_gather(precond, "example", axis=1, tiled=True)
    all_queries = lax.all_gather(queries, "example", axis=1, tiled=True)
    ready = jnp.einsum(
        "lqr,lrs->lqs",
        all_queries,
        full_matrix,
        precision=lax.Precision.HIGHEST,
        preferred_element_type=jnp.float32,
    )
    moved = jnp.einsum(
        "ler,lrs->les",
        store,
        full_matrix,
        precision=lax.Precision.HIGHEST,
        preferred_element_type=jnp.float32,
    )
    size_terms = jnp.sum(moved * store, axis=(0, 2))
    own_scores = lax.psum_scatter(
        jnp.einsum(
            "lqr,ler->qe",
            ready,
            store,
            precision=lax.Precision.HIGHEST,
            preferred_element_type=jnp.float32,
        ),
        "layer",
        scatter_dimension=0,
        tiled=True,
    )
    sizes_sq = lax.psum(size_terms, "layer")
    return own_scores / jnp.sqrt(sizes_sq)[None, :]


def solution(mesh):
    in_specs = (
        P("layer", "example", None),
        P("layer", "example", None),
        P("layer", "example", None),
    )
    out_specs = P("layer", "example")
    return jax.shard_map(shards, mesh=mesh, in_specs=in_specs, out_specs=out_specs, check_vma=False)
```

profile of v0, /device:TPU:0, one launch (start us, length us, event | category | flops | bytes accessed | tf_op | source)
XLA Modules:
  0.0 256.3 jit_solution(2458823560508071457)
XLA Ops:
  6.5 0.0 all-gather.3.cloned.1.call-start
  6.5 0.7 all-gather.3.cloned.1.call-update
  7.3 0.0 all-gather.5.cloned.1.call-start
  7.3 0.7 all-gather.5.cloned.1.call-update
  8.0 0.0 reduce-scatter.2.cloned.1.call-start
  8.1 49.0 %all-gather.3.cloned.1.call-done = f32[1,256,1024]{2,1,0:T(8,128)} async-done(((f32[1,16,1024]{2,1,0:T(8,128)}), f32[1,256,1024]{2,1,0:T(8,128)}) %all-gather.3.cloned.1.call-update) | async-done | bytes 1048592 | tf_op jit(solution)/shard_map/all_gather | solution.py:9
  57.0 56.4 %all-gather.5.cloned.1.call-done = f32[1,1024,1024]{2,1,0:T(8,128)} async-done(((f32[1,64,1024]{2,1,0:T(8,128)}), f32[1,1024,1024]{2,1,0:T(8,128)}) %all-gather.5.cloned.1.call-update) | async-done | bytes 4194320 | tf_op jit(solution)/shard_map/all_gather | solution.py:8
  113.4 6.0 %fusion.8 = f32[256,1024]{1,0:T(8,128)S(1)} fusion(f32[1,1024,1024]{2,1,0:T(8,128)} %all-gather.5.cloned.1.call-done, f32[1,256,1024]{2,1,0:T(8,128)} %all-gather.3.cloned.1.call-done), kind=kOutput, calls=%fused_computation.7 | convolution fusion | flops 3221225472 | bytes 6291456 | tf_op jit(solution)/shard_map/lqr,lrs->lqs/dot_general | solution.py:10
  119.4 18.0 %fusion.3 = f32[256,4096]{1,0:T(8,128)} fusion(f32[256,1024]{1,0:T(8,128)S(1)} %fusion.8, f32[1,4096,1024]{2,1,0:T(8,128)} %param.5), kind=kOutput, calls=%fused_computation.4 | convolution fusion | flops 12884901888 | bytes 22020096 | tf_op jit(solution)/shard_map/lqr,ler->qe/dot_general | solution.py:26
  137.5 0.0 reduce-scatter.2.cloned.1.call-update
  137.5 17.6 %copy.4 = f32[1,4096,1024]{1,2,0:T(8,128)} copy(f32[1,4096,1024]{2,1,0:T(8,128)} %param.5) | data formatting | bytes 33554432 | tf_op args[2]
  155.1 59.3 %fusion = f32[4096]{0:T(1024)S(1)} fusion(f32[1,4096,1024]{1,2,0:T(8,128)} %copy.4, f32[1,4096,1024]{2,1,0:T(8,128)} %param.5, f32[1,1024,1024]{2,1,0:T(8,128)} %all-gather.5.cloned.1.call-done), kind=kOutput, calls=%fused_computation.1 | convolution fusion | flops 51547992064 | bytes 37765120 | tf_op jit(solution)/shard_map/ler,lrs->les/dot_general | solution.py:17
  214.4 33.4 %psum.7 = f32[4096]{0:T(1024)S(1)} all-reduce(f32[4096]{0:T(1024)S(1)} %fusion), channel_id=1, replica_groups=mesh['layer'=8,'example'=16] {'layer'}, use_global_device_ids=true, to_apply=%region_2.0 | all-reduce | flops 4096 | bytes 32768 | tf_op jit(solution)/shard_map/psum | solution.py:37
  247.9 0.0 reduce-scatter.2.cloned.1.call-done
  247.9 1.9 broadcast_divide_fusion
  (1 shorter events, 0.0 us)
Async XLA Ops:
  6.5 50.5 %all-gather.3.cloned.1.call-start = ((), (), s32[]{:S(2)}) async-start(), calls=%async_computation.1 | async-start | bytes 1114112 | tf_op jit(solution)/shard_map/all_gather | solution.py:9
  7.3 106.2 %all-gather.5.cloned.1.call-start = ((), (), s32[]{:S(2)}) async-start(), calls=%async_computation.2 | async-start | bytes 4456448 | tf_op jit(solution)/shard_map/all_gather | solution.py:8
  8.0 239.9 %reduce-scatter.2.cloned.1.call-start = ((), (), s32[]{:S(2)}) async-start(), calls=%async_computation.3 | async-start | bytes 4718592 | tf_op jit(solution)/shard_map/reduce_scatter | solution.py:25
Sparse Core Ops, SparseCore 0:
  9.8 47.1 all-gather.2
  59.5 53.8 all-gather.4
  137.6 51.1 reduce-scatter.1
where the time goes:
time: 257 us; the launch traced here: 256 us
  waiting for transfers between devices  107 us (42%)
  matrix products  83.3 us (32%)
  blocking collectives  33.4 us (13%)
  local copies, waits for them, and re-layouts  17.6 us (7%)
  between operations  13.1 us (5%)
    dot_general x1, matrix products, shards(): jnp.einsum('ler,lrs->les', store, full_matrix, precision=lax.Precision.HI...  59.3 us
    all_gather x1, waiting for transfers between devices, shards(): full_matrix = lax.all_gather(precond, 'example', axis=1, tiled=True)  56.4 us
    all_gather x1, waiting for transfers between devices, shards(): all_queries = lax.all_gather(queries, 'example', axis=1, tiled=True)  49 us
    psum x1, blocking collectives, shards(): sizes_sq = lax.psum(size_terms, 'layer')  33.4 us
    dot_general x1, matrix products, shards(): jnp.einsum('lqr,ler->qe', ready, store, precision=lax.Precision.HIGHEST,...  18 us
    unnamed x1, local copies, waits for them, and re-layouts  17.6 us
    dot_general x1, matrix products, shards(): jnp.einsum('lqr,lrs->lqs', all_queries, full_matrix, precision=lax.Precis...  5.97 us
  transfers between devices with their start and end apart: 3, of which 2 were waited for; matrix products, arithmetic and copies ran while one was open for 30% of the time, Pallas kernels for 0%

commit v1 on v0

v1 whole, which is shorter than its diff:
```python
import functools

import jax
import jax.numpy as jnp
from jax import lax
from jax.experimental import pallas as pl
from jax.experimental.pallas import tpu as pltpu
from jax.sharding import PartitionSpec as P

R = 1024
Q = 256
ROWS = 64
QROWS = 16
PIECE = ROWS + QROWS
TILE = 1024
SPLIT = (2048, 2048)
BF16 = jnp.bfloat16
F32 = jnp.float32
LIMIT = 20 * 2**20
nt_dot = functools.partial(
    lax.dot_general, dimension_numbers=(((1,), (1,)), ((), ())), preferred_element_type=F32
)
VMEM = pl.BlockSpec(memory_space=pltpu.VMEM)
SMEM = pl.BlockSpec(memory_space=pltpu.SMEM)


def example_permute(x, to):
    pairs = []
    for x_hi in range(2):
        for y in range(4):
            for core in range(2):
                a, b, c = to(x_hi, y, core)
                pairs.append((x_hi * 8 + y * 2 + core, a * 8 + (b % 4) * 2 + c))
    return lax.ppermute(x, "example", pairs)


def layer_permute(x, to):
    pairs = []
    for x_lo in range(2):
        for z in range(4):
            a, b = to(x_lo, z)
            pairs.append((x_lo * 4 + z, a * 4 + b % 4))
    return lax.ppermute(x, "layer", pairs)


def swap_core(x):
    return example_permute(x, lambda x_hi, y, core: (x_hi, y, 1 - core))


def z_up(x):
    return layer_permute(x, lambda x_lo, z: (x_lo, z + 1))


def z_down(x):
    return layer_permute(x, lambda x_lo, z: (x_lo, z - 1))


def swap_x(x):
    return layer_permute(x, lambda x_lo, z: (1 - x_lo, z))


NEAR = [(0, 0, 0, 0), (0, PIECE, 1, 0), (1, 0, 0, 1), (1, PIECE, 1, 1)]
FAR = [(0, 0, 0, 0), (1, 0, 1, 0), (2, 0, 0, 1), (3, 0, 1, 1)]


def tie(*arrays):
    return lax.optimization_barrier(arrays)


def split(blocks, bufs, x_hi, core, hi_ref, lo_ref):
    for b, off, x_flip, core_flip in blocks:
        at = ((x_hi + x_flip) % 2) * 2 + (core + core_flip) % 2
        rows = pl.ds(pl.multiple_of(at * ROWS, ROWS), ROWS)
        block = bufs[b][off : off + ROWS, :]
        hi = block.astype(BF16)
        hi_ref[rows, :] = hi
        lo_ref[rows, :] = (block - hi.astype(F32)).astype(BF16)


def add_sizes(y_shifts, y, s_ref, matrices, o_ref):
    @pl.loop(0, o_ref.shape[1] // TILE)
    def _(i):
        rows = pl.ds(pl.multiple_of(i * TILE, TILE), TILE)
        sh = s_ref[rows, :].astype(BF16)
        total = 0.0
        for y_shift, (hi_ref, lo_ref) in zip(y_shifts, matrices):
            moved = nt_dot(sh, hi_ref[...]) + nt_dot(sh, lo_ref[...])
            first = pl.multiple_of(((y + y_shift + 4) % 4) * 128, 128)
            for half in range(2):
                cols = pl.ds(first + half * 512, 128)
                own = s_ref[rows, cols]
                weight = 2.0 * own - own.astype(BF16).astype(F32)
                total += moved[:, half * 128 : half * 128 + 128] * weight
        o_ref[:, rows] = jnp.sum(total.T, axis=0, keepdims=True)


def part_kernel(blocks, y_shift, n, where_ref, *refs):
    bufs, (s_ref, hi_ref, lo_ref, o_ref) = refs[:n], refs[n:]
    me = where_ref[0]
    split(blocks, bufs, me // 8, me % 2, hi_ref, lo_ref)
    add_sizes([y_shift], (me // 2) % 4, s_ref, [(hi_ref, lo_ref)], o_ref)


def part_sizes(where, part, store):
    y_shift, buffers, blocks = part
    examples = store.shape[0]
    return pl.pallas_call(
        functools.partial(part_kernel, blocks, y_shift, len(buffers)),
        in_specs=[SMEM] + [VMEM] * (len(buffers) + 1),
        out_specs=[VMEM] * 3,
        out_shape=[jax.ShapeDtypeStruct((256, R), BF16)] * 2 + [jax.ShapeDtypeStruct((1, examples), F32)],
        compiler_params=pltpu.CompilerParams(vmem_limit_bytes=LIMIT),
        cost_estimate=pl.CostEstimate(
            flops=8 * 256 * R * examples, bytes_accessed=4 * R * examples, transcendentals=0
        ),
    )(where, *buffers, store)


def rest_kernel(y_shifts, where_ref, *refs):
    mats, (s_ref, o_ref) = refs[:-2], refs[-2:]
    pairs = [(mats[2 * k], mats[2 * k + 1]) for k in range(len(y_shifts))]
    add_sizes(y_shifts, (where_ref[0] // 2) % 4, s_ref, pairs, o_ref)


def rest_sizes(where, y_shifts, matrices, store):
    examples = store.shape[0]
    return pl.pallas_call(
        functools.partial(rest_kernel, y_shifts),
        in_specs=[SMEM] + [VMEM] * (len(matrices) + 1),
        out_specs=VMEM,
        out_shape=jax.ShapeDtypeStruct((1, examples), F32),
        compiler_params=pltpu.CompilerParams(vmem_limit_bytes=LIMIT),
        cost_estimate=pl.CostEstimate(
            flops=8 * 256 * len(y_shifts) * R * examples, bytes_accessed=4 * R * examples, transcendentals=0
        ),
    )(where, *matrices, store)


SLOTS = (6, 7, 4, 1, 0, 2, 3, 5)


def ready_kernel(parts, n, where_ref, *refs):
    ins, (rh_ref, rl_ref, *made), q_ref = refs[:n], refs[n:-1], refs[-1]
    me, x_lo, z = where_ref[0], where_ref[1], where_ref[2]
    x_hi, y, core = me // 8, (me // 2) % 4, me % 2
    matrices = []
    for y_shift, first, count, blocks, ready_made in parts:
        bufs = ins[first : first + count]
        if ready_made:
            matrices.append((y_shift, ins[first + count], ins[first + count + 1]))
        else:
            hi_ref, lo_ref, *made = made
            split(blocks, bufs, x_hi, core, hi_ref, lo_ref)
            matrices.append((y_shift, hi_ref, lo_ref))
        for b, off, x_flip, core_flip in blocks:
            to_z, to_x = (y + y_shift + 4) % 4, (x_hi + x_flip) % 2
            code = ((to_z - z + 4) % 4) * 2 + (to_x + x_lo) % 2
            slot = sum(jnp.where(code == k, s, 0) for k, s in enumerate(SLOTS))
            at = slot * 2 + (core + core_flip) % 2
            rows = pl.ds(pl.multiple_of(at * QROWS, QROWS), QROWS)
            q_ref[rows, :] = bufs[b][off + ROWS : off + PIECE, :]
    q = q_ref[...]
    qh = q.astype(BF16)
    ql = (q - qh.astype(F32)).astype(BF16)
    for y_shift, hi_ref, lo_ref in matrices:
        ready = nt_dot(qh, hi_ref[...]) + nt_dot(qh, lo_ref[...]) + nt_dot(ql, hi_ref[...])
        high = ready.astype(BF16)
        low = (ready - high.astype(F32)).astype(BF16)
        start = pl.multiple_of(((y + y_shift + 4) % 4) * 128, 128)
        for half in range(2):
            cols = pl.ds(start + half * 512, 128)
            rh_ref[:, cols] = high[:, half * 128 : half * 128 + 128]
            rl_ref[:, cols] = low[:, half * 128 : half * 128 + 128]


def ready_queries(where, parts, matrices):
    refs, rows, missing = [], [], 0
    for (y_shift, buffers, blocks), made in zip(parts, matrices):
        rows.append((y_shift, len(refs), len(buffers), blocks, bool(made)))
        refs += list(buffers) + list(made)
        missing += not made
    shapes = [(Q, R)] * 2 + [(256, R)] * (2 * missing)
    return pl.pallas_call(
        functools.partial(ready_kernel, rows, len(refs)),
        in_specs=[SMEM] + [VMEM] * len(refs),
        out_specs=[VMEM] * len(shapes),
        out_shape=[jax.ShapeDtypeStruct(shape, BF16) for shape in shapes],
        scratch_shapes=[pltpu.VMEM((Q, R), F32)],
        compiler_params=pltpu.CompilerParams(vmem_limit_bytes=LIMIT),
        cost_estimate=pl.CostEstimate(flops=6 * Q * R * R, bytes_accessed=2**20, transcendentals=0),
    )(where, *refs)


CUTS = (64, 64, 32, 32, 64)


def raw_kernel(first, rh_ref, rl_ref, s_ref, *outs):
    @pl.loop(0, outs[0].shape[1] // TILE)
    def _(i):
        rows = pl.ds(pl.multiple_of(first + i * TILE, TILE), TILE)
        cols = pl.ds(pl.multiple_of(i * TILE, TILE), TILE)
        s = s_ref[rows, :]
        sh = s.astype(BF16)
        sl = (s - sh.astype(F32)).astype(BF16)
        raw = nt_dot(rh_ref[...], sh) + nt_dot(rh_ref[...], sl) + nt_dot(rl_ref[...], sh)
        at = 0
        for n, ref in zip(CUTS, outs):
            ref[:, cols] = raw[at : at + n]
            at += n


def raw_scores(rh, rl, store, first, examples):
    return pl.pallas_call(
        functools.partial(raw_kernel, first),
        in_specs=[VMEM] * 3,
        out_specs=[VMEM] * len(CUTS),
        out_shape=[jax.ShapeDtypeStruct((n, examples), F32) for n in CUTS],
        compiler_params=pltpu.CompilerParams(vmem_limit_bytes=LIMIT),
        cost_estimate=pl.CostEstimate(
            flops=8 * Q * R * examples, bytes_accessed=4 * (R + Q) * examples, transcendentals=0
        ),
    )(rh, rl, store)


def shards(queries, precond, store):
    layer = lax.axis_index("layer")
    where = jnp.stack([lax.axis_index("example"), layer // 4, layer % 4]).astype(jnp.int32)
    store = store[0]

    piece = jnp.concatenate([precond[0], queries[0]], axis=0)
    other = example_permute(piece, lambda x_hi, y, core: (1 - x_hi, y, core))
    pair = jnp.concatenate([piece, other], axis=0)
    left = example_permute(pair, lambda x_hi, y, core: (x_hi, y + 1, core))
    right = example_permute(pair, lambda x_hi, y, core: (x_hi, y - 1, core))
    own = (0, [pair, swap_core(pair)], NEAR)
    own_hi, own_lo, own_part = part_sizes(where, own, store)
    left, right, own_part = tie(left, right, own_part)
    far0 = example_permute(left[:PIECE], lambda x_hi, y, core: (x_hi, y + 1, core))
    far1 = example_permute(right[PIECE:], lambda x_hi, y, core: (x_hi, y - 1, core))
    below = (-1, [left, swap_core(left)], NEAR)
    below_hi, below_lo, below_part = part_sizes(where, below, store)
    above = (1, [right, swap_core(right)], NEAR)
    far0, far1, below_part = tie(far0, far1, below_part)
    across = (2, [far0, far1, swap_core(far0), swap_core(far1)], FAR)
    rh, rl, *rest = ready_queries(
        where, [own, below, above, across], [(own_hi, own_lo), (below_hi, below_lo), (), ()]
    )

    blocks, first = [], 0
    for examples in SPLIT:
        blocks.append(raw_scores(rh, rl, store, first, examples))
        rh = tie(rh, blocks[-1][-1])[0]
        first += examples
    (up1, down1, up2, down2, mine), (up1b, down1b, up2b, down2b, mineb) = blocks
    from_below, from_above = z_up(up1), z_down(down1)
    from_belowb, from_aboveb = z_up(up1b), z_down(down1b)
    *rest, from_below, from_above = tie(*rest, from_below, from_above)
    rest_part = rest_sizes(where, [1, 2], rest, store)
    last_below, last_above = z_up(up2 + from_below[:32]), z_down(down2 + from_above[:32])
    here = mine[:32] + from_above[32:] + last_below
    there = mine[32:] + from_below[32:] + last_above
    scores = [here + swap_x(there)]
    sizes_sq = own_part + below_part + rest_part
    sizes_sq, from_belowb, from_aboveb = tie(sizes_sq, from_belowb, from_aboveb)
    last_below, last_above = z_up(up2b + from_belowb[:32]), z_down(down2b + from_aboveb[:32])
    here = mineb[:32] + from_aboveb[32:] + last_below
    there = mineb[32:] + from_belowb[32:] + last_above
    scores.append(here + swap_x(there))

    sizes_sq = sizes_sq + z_up(sizes_sq) + z_down(sizes_sq) + layer_permute(sizes_sq, lambda x, z: (x, z + 2))
    root = jnp.sqrt(sizes_sq + swap_x(sizes_sq))
    return jnp.concatenate(scores, axis=1) / root


def solution(mesh):
    in_specs = (
        P("layer", "example", None),
        P("layer", "example", None),
        P("layer", "example", None),
    )
    out_specs = P("layer", "example")
    return jax.shard_map(shards, mesh=mesh, in_specs=in_specs, out_specs=out_specs, check_vma=False)
```

time: 257 us -> 111 us (0.43)
  matrix products: 83.3 us -> 0 us
  waiting for transfers between devices: 107 us -> 34.2 us
  Pallas kernels: 0 us -> 33.7 us
  starting transfers between devices: 0.08 us -> 33.6 us
  blocking collectives: 33.4 us -> 0 us
  between operations: 13.1 us -> 0.15 us
  local copies, waits for them, and re-layouts: 17.6 us -> 5.82 us
    all_gather x2 -> x0, waiting for transfers between devices: 105 us -> none  [the longest x1 56.4 us: shards(): full_matrix = lax.all_gather(precond, 'example', axis=1, tiled=True)]
    dot_general x3 -> x0, matrix products: 83.3 us -> none  [the longest x1 59.3 us: shards(): jnp.einsum('ler,lrs->les', store, full_matrix, precision=lax.Precision.HI...]
    ppermute x0 -> x24, waiting for transfers between devices: none -> 34.2 us  [the longest x14 17.5 us: layer_permute(): return lax.ppermute(x, 'layer', pairs)]
    pallas_call x0 -> x6, Pallas kernels: none -> 33.7 us  [the longest x2 12.5 us: part_sizes(): pl.pallas_call(functools.partial(part_kernel, blocks, y_shift, len(buffer...]
    ppermute x0 -> x24, starting transfers between devices: none -> 33.6 us  [the longest x14 22.7 us: layer_permute(): return lax.ppermute(x, 'layer', pairs)]
    psum x1 -> x0, blocking collectives: 33.4 us -> none  [shards(): sizes_sq = lax.psum(size_terms, 'layer')]
    unnamed x1 -> x4, local copies, waits for them, and re-layouts: 17.6 us -> 5.77 us
  transfers between devices with their start and end apart: 3 -> 24, of which waited for: 2 -> 13; matrix products, arithmetic and copies ran while one was open for 30% -> 0% of each run, Pallas kernels for 0% -> 24%
where the time goes in v1:
time: 111 us
  waiting for transfers between devices  34.2 us (31%)
  Pallas kernels  33.7 us (30%)
  starting transfers between devices  33.6 us (30%)
  local copies, waits for them, and re-layouts  5.82 us (5%)
  other arithmetic  3.39 us (3%)
    ppermute x14, starting transfers between devices, layer_permute(): return lax.ppermute(x, 'layer', pairs)  22.7 us
    ppermute x14, waiting for transfers between devices, layer_permute(): return lax.ppermute(x, 'layer', pairs)  17.5 us
    ppermute x10, waiting for transfers between devices, example_permute(): return lax.ppermute(x, 'example', pairs)  16.7 us
    pallas_call x2, Pallas kernels, part_sizes(): pl.pallas_call(functools.partial(part_kernel, blocks, y_shift, len(buffer...  12.5 us
    ppermute x10, starting transfers between devices, example_permute(): return lax.ppermute(x, 'example', pairs)  10.9 us
    pallas_call x1, Pallas kernels, rest_sizes(): pl.pallas_call(functools.partial(rest_kernel, y_shifts), in_specs=[SMEM]...  10.7 us
    pallas_call x2, Pallas kernels, raw_scores(): pl.pallas_call(functools.partial(raw_kernel, first), in_specs=[VMEM] * 3,...  7.36 us
    unnamed x4, local copies, waits for them, and re-layouts  5.77 us
  transfers between devices with their start and end apart: 24, of which 13 were waited for; matrix products, arithmetic and copies ran while one was open for 0% of the time, Pallas kernels for 24%

profile of v1, /device:TPU:0, one launch (start us, length us, event | category | flops | bytes accessed | tf_op | source)
XLA Modules:
  0.0 110.8 jit_solution(5015075723037754061)
XLA Ops:
  0.0 1.0 pad_maximum_fusion.1
  1.0 3.2 %collective-permute-start = (f32[80,1024]{1,0:T(8,128)S(1)}, f32[80,1024]{1,0:T(8,128)S(1)}, u32[]{:S(2)}, u32[]{:S(2)}) collective-permute-start(f32[80,1024]{1,0:T(8,128)S(1)} %pad_maximum_fusion.1), channel_id=1, source_target_pairs={{0,8},{1,9},{2,10},{3,11},{4,12},{5,13},{6,14},{7,15},{8,0},{9,1},... | collective-permute-start | bytes 983048 | tf_op jit(solution)/shard_map/ppermute | solution.py:34
  4.2 7.7 %collective-permute-done = f32[80,1024]{1,0:T(8,128)S(1)} collective-permute-done((f32[80,1024]{1,0:T(8,128)S(1)}, f32[80,1024]{1,0:T(8,128)S(1)}, u32[]{:S(2)}, u32[]{:S(2)}) %collective-permute-start) | collective-permute-done | bytes 327712 | tf_op jit(solution)/shard_map/ppermute | solution.py:34
  11.9 1.0 pad_maximum_fusion.refs_0_
  13.0 0.1 collective-permute-start.1
  13.1 0.1 pad_add_fusion.where_ref
  13.1 3.2 %collective-permute-start.3 = (f32[160,1024]{1,0:T(8,128)S(1)}, f32[160,1024]{1,0:T(8,128)S(1)}, u32[]{:S(2)}, u32[]{:S(2)}) collective-permute-start(f32[160,1024]{1,0:T(8,128)S(1)} %pad_maximum_fusion.refs_0_), channel_id=1, source_target_pairs={{0,6},{1,7},{2,0},{3,1},{4,2},{5,3},{6,4},{7,5},{8,14},{9,15},{10,... | collective-permute-start | bytes 1966088 | tf_op jit(solution)/shard_map/ppermute | solution.py:34
  16.4 0.0 collective-permute-start.2
  16.4 0.0 collective-permute-done.1.refs_1_
  16.4 5.8 %copy-done = f32[1,4096,1024]{2,1,0:T(8,128)S(1)} copy-done((f32[1,4096,1024]{2,1,0:T(8,128)S(1)}, f32[1,4096,1024]{2,1,0:T(8,128)}, u32[]{:S(2)}) %copy-start) | copy-done | bytes 16777240
  22.2 6.2 %shard_map.37 = (bf16[256,1024]{1,0:T(8,128)(2,1)S(1)}, bf16[256,1024]{1,0:T(8,128)(2,1)S(1)}, f32[1,4096]{1,0:T(1,128)S(1)}) custom-call(s32[3]{0:T(128)S(1)} %pad_add_fusion.where_ref, f32[160,1024]{1,0:T(8,128)S(1)} %pad_maximum_fusion.refs_0_, f32[160,1024]{1,0:T(8,128)S(1)} %collective-permute-done.1.refs_1_, f32[4096,1024]{1,0:T(8,128)S(1)} %bitcast.7), custom_call_target="tpu_custom_call" | custom-call | flops 8589934592 | bytes 16777216 | tf_op jit(solution)/shard_map/pallas_call | solution.py:107
  28.4 2.6 %collective-permute-done.3.refs_8_ = f32[160,1024]{1,0:T(8,128)S(1)} collective-permute-done((f32[160,1024]{1,0:T(8,128)S(1)}, f32[160,1024]{1,0:T(8,128)S(1)}, u32[]{:S(2)}, u32[]{:S(2)}) %collective-permute-start.3) | collective-permute-done | bytes 655392 | tf_op jit(solution)/shard_map/ppermute | solution.py:34
  31.0 3.4 %collective-permute-done.2.refs_0_.refs_4_ = f32[160,1024]{1,0:T(8,128)S(1)} collective-permute-done((f32[160,1024]{1,0:T(8,128)S(1)}, f32[160,1024]{1,0:T(8,128)S(1)}, u32[]{:S(2)}, u32[]{:S(2)}) %collective-permute-start.2) | collective-permute-done | bytes 655392 | tf_op jit(solution)/shard_map/ppermute | solution.py:34
  34.4 0.0 collective-permute-start.4
  34.5 0.6 collective-permute-start.5
  35.1 0.0 collective-permute-start.6
  35.1 3.2 %collective-permute-start.7 = (f32[80,1024]{1,0:T(8,128)S(1)}, f32[80,1024]{1,0:T(8,128)S(1)}, u32[]{:S(2)}, u32[]{:S(2)}) collective-permute-start(f32[80,1024]{1,0:T(8,128)S(1)} %slice.43), channel_id=1, source_target_pairs={{0,6},{1,7},{2,0},{3,1},{4,2},{5,3},{6,4},{7,5},{8,14},{9,15},{10,... | collective-permute-start | bytes 983048 | tf_op jit(solution)/shard_map/ppermute | solution.py:34
  38.3 0.0 collective-permute-done.4.refs_1_.refs_5_
  38.3 0.0 copy-done.1
  38.3 6.3 %shard_map.38 = (bf16[256,1024]{1,0:T(8,128)(2,1)S(1)}, bf16[256,1024]{1,0:T(8,128)(2,1)S(1)}, f32[1,4096]{1,0:T(1,128)S(1)}) custom-call(s32[3]{0:T(128)S(1)} %pad_add_fusion.where_ref, f32[160,1024]{1,0:T(8,128)S(1)} %collective-permute-done.2.refs_0_.refs_4_, f32[160,1024]{1,0:T(8,128)S(1)} %collective-permute-done.4.refs_1_.refs_5_, f32[4096,1024]{1,0:T(8,128)S(1)} %bitcast.8), custom_call_target="tpu_custom_call" | custom-call | flops 8589934592 | bytes 16777216 | tf_op jit(solution)/shard_map/pallas_call | solution.py:107
  44.6 1.3 %collective-permute-done.6.refs_10_ = f32[80,1024]{1,0:T(8,128)S(1)} collective-permute-done((f32[80,1024]{1,0:T(8,128)S(1)}, f32[80,1024]{1,0:T(8,128)S(1)}, u32[]{:S(2)}, u32[]{:S(2)}) %collective-permute-start.6) | collective-permute-done | bytes 327712 | tf_op jit(solution)/shard_map/ppermute | solution.py:34
  46.0 0.0 collective-permute-done.7.refs_11_
  46.0 0.0 collective-permute-start.8
  46.0 0.5 collective-permute-start.9
  46.5 0.0 collective-permute-done.5.refs_9_
  46.5 1.1 %collective-permute-done.8.refs_12_ = f32[80,1024]{1,0:T(8,128)S(1)} collective-permute-done((f32[80,1024]{1,0:T(8,128)S(1)}, f32[80,1024]{1,0:T(8,128)S(1)}, u32[]{:S(2)}, u32[]{:S(2)}) %collective-permute-start.8) | collective-permute-done | bytes 327712 | tf_op jit(solution)/shard_map/ppermute | solution.py:34
  47.6 0.5 collective-permute-done.9.refs_13_
  48.1 3.1 %shard_map.39 = (bf16[256,1024]{1,0:T(8,128)(2,1)S(1)}, bf16[256,1024]{1,0:T(8,128)(2,1)S(1)}, bf16[256,1024]{1,0:T(8,128)(2,1)S(1)}, bf16[256,1024]{1,0:T(8,128...) custom-call(s32[3]{0:T(128)S(1)} %pad_add_fusion.where_ref, ...), custom_call_target="tpu_custom_call" | custom-call | flops 1610612736 | bytes 1048576 | tf_op jit(solution)/shard_map/pallas_call | solution.py:183
  51.2 3.7 %shard_map.40 = (f32[64,2048]{1,0:T(8,128)S(1)}, f32[64,2048]{1,0:T(8,128)S(1)}, f32[32,2048]{1,0:T(8,128)S(1)}, f32[32,2048]{1,0:T(8,128)S(1)}, f32[64,2048]{1,0:T(8,128)S(1)}) custom-call(bf16[256,1024]{1,0:T(8,128)(2,1)S(1)} %get-tuple-element.66.rh_ref, bf16[256,1024]{1,0:T(8,128)(2,1)S(1)} %get-tuple-element.54.rl_ref, f32[4096,1024]{1,0:T(8,128)S(1)} %bitcast.9), custom_call_target="tpu_custom_call" | custom-call | flops 4294967296 | bytes 10485760 | tf_op jit(solution)/shard_map/pallas_call | solution.py:213
  54.9 2.0 %collective-permute-start.10 = (f32[64,2048]{1,0:T(8,128)S(1)}, f32[64,2048]{1,0:T(8,128)S(1)}, u32[]{:S(2)}, u32[]{:S(2)}) collective-permute-start(f32[64,2048]{1,0:T(8,128)S(1)} %get-tuple-element.60), channel_id=1, source_target_pairs={{0,16},{16,32},{32,48},{48,0},{64,80},{80,96},{96,112},{112,64},{1... | collective-permute-start | bytes 1572872 | tf_op jit(solution)/shard_map/ppermute | solution.py:43
  56.8 2.2 %collective-permute-start.11 = (f32[64,2048]{1,0:T(8,128)S(1)}, f32[64,2048]{1,0:T(8,128)S(1)}, u32[]{:S(2)}, u32[]{:S(2)}) collective-permute-start(f32[64,2048]{1,0:T(8,128)S(1)} %get-tuple-element.61), channel_id=1, source_target_pairs={{0,48},{16,0},{32,16},{48,32},{64,112},{80,64},{96,80},{112,96},{1... | collective-permute-start | bytes 1572872 | tf_op jit(solution)/shard_map/ppermute | solution.py:43
  59.0 3.7 %shard_map.41 = (f32[64,2048]{1,0:T(8,128)S(1)}, f32[64,2048]{1,0:T(8,128)S(1)}, f32[32,2048]{1,0:T(8,128)S(1)}, f32[32,2048]{1,0:T(8,128)S(1)}, f32[64,2048]{1,0:T(8,128)S(1)}) custom-call(bf16[256,1024]{1,0:T(8,128)(2,1)S(1)} %get-tuple-element.66.rh_ref, bf16[256,1024]{1,0:T(8,128)(2,1)S(1)} %get-tuple-element.54.rl_ref, f32[4096,1024]{1,0:T(8,128)S(1)} %bitcast.10), custom_call_target="tpu_custom_call" | custom-call | flops 4294967296 | bytes 10485760 | tf_op jit(solution)/shard_map/pallas_call | solution.py:213
  62.7 0.1 collective-permute-start.15
  62.8 3.2 %collective-permute-start.16 = (f32[64,2048]{1,0:T(8,128)S(1)}, f32[64,2048]{1,0:T(8,128)S(1)}, u32[]{:S(2)}, u32[]{:S(2)}) collective-permute-start(f32[64,2048]{1,0:T(8,128)S(1)} %get-tuple-element.75), channel_id=1, source_target_pairs={{0,48},{16,0},{32,16},{48,32},{64,112},{80,64},{96,80},{112,96},{1... | collective-permute-start | bytes 1572872 | tf_op jit(solution)/shard_map/ppermute | solution.py:43
  66.0 5.6 %collective-permute-done.10 = f32[64,2048]{1,0:T(8,128)S(1)} collective-permute-done((f32[64,2048]{1,0:T(8,128)S(1)}, f32[64,2048]{1,0:T(8,128)S(1)}, u32[]{:S(2)}, u32[]{:S(2)}) %collective-permute-start.10) | collective-permute-done | bytes 524320 | tf_op jit(solution)/shard_map/ppermute | solution.py:43
  71.7 0.0 collective-permute-done.11
  71.7 10.7 %shard_map.42 = f32[1,4096]{1,0:T(1,128)S(1)} custom-call(s32[3]{0:T(128)S(1)} %pad_add_fusion.where_ref, bf16[256,1024]{1,0:T(8,128)(2,1)S(1)} %get-tuple-element.70.refs_0_, bf16[256,1024]{1,0:T(8,128)(2,1)S(1)} %get-tuple-element.71.refs_1_, bf16[256,1024]{1,0:T(8,128)(2,1)S(1)} %get-tuple-element.72.refs_2_, ...), custom_call_target="tpu_custom_call" | custom-call | flops 17179869184 | bytes 16777216 | tf_op jit(solution)/shard_map/pallas_call | solution.py:127
  82.4 0.0 collective-permute-done.15
  82.4 0.0 collective-permute-done.16
  82.4 3.6 %collective-permute-start.22 = (f32[1,4096]{1,0:T(1,128)S(1)}, f32[1,4096]{1,0:T(1,128)S(1)}, u32[]{:S(2)}, u32[]{:S(2)}) collective-permute-start(f32[1,4096]{1,0:T(1,128)S(1)} %add_add_fusion.5), channel_id=1, source_target_pairs={{0,32},{16,48},{32,0},{48,16},{64,96},{80,112},{96,64},{112,80},{1... | collective-permute-start | bytes 49160 | tf_op jit(solution)/shard_map/ppermute | solution.py:43
  86.1 1.0 collective-permute-start.21
  87.1 1.0 collective-permute-start.20
  88.1 2.3 %collective-permute-start.13 = (f32[32,2048]{1,0:T(8,128)S(1)}, f32[32,2048]{1,0:T(8,128)S(1)}, u32[]{:S(2)}, u32[]{:S(2)}) collective-permute-start(f32[32,2048]{1,0:T(8,128)S(1)} %slice_add_fusion.2), channel_id=1, source_target_pairs={{0,48},{16,0},{32,16},{48,32},{64,112},{80,64},{96,80},{112,96},{1... | collective-permute-start | bytes 786440 | tf_op jit(solution)/shard_map/ppermute | solution.py:43
  90.4 0.0 collective-permute-done.22
  90.4 0.0 collective-permute-done.21
  90.4 1.6 %collective-permute-done.20 = f32[1,4096]{1,0:T(1,128)S(1)} collective-permute-done((f32[1,4096]{1,0:T(1,128)S(1)}, f32[1,4096]{1,0:T(1,128)S(1)}, u32[]{:S(2)}, u32[]{:S(2)}) %collective-permute-start.20) | collective-permute-done | bytes 16416 | tf_op jit(solution)/shard_map/ppermute | solution.py:43
  92.0 1.6 %collective-permute-start.23 = (f32[1,4096]{1,0:T(1,128)S(1)}, f32[1,4096]{1,0:T(1,128)S(1)}, u32[]{:S(2)}, u32[]{:S(2)}) collective-permute-start(f32[1,4096]{1,0:T(1,128)S(1)} %add_add_fusion.4), channel_id=1, source_target_pairs={{0,64},{16,80},{32,96},{48,112},{64,0},{80,16},{96,32},{112,48},{1... | collective-permute-start | bytes 49160 | tf_op jit(solution)/shard_map/ppermute | solution.py:43
  93.6 0.2 collective-permute-start.18
  93.9 2.1 %collective-permute-done.23 = f32[1,4096]{1,0:T(1,128)S(1)} collective-permute-done((f32[1,4096]{1,0:T(1,128)S(1)}, f32[1,4096]{1,0:T(1,128)S(1)}, u32[]{:S(2)}, u32[]{:S(2)}) %collective-permute-start.23) | collective-permute-done | bytes 16416 | tf_op jit(solution)/shard_map/ppermute | solution.py:43
  96.0 0.6 collective-permute-done.13
  96.6 0.1 slice_add_fusion.3
  96.7 1.6 %collective-permute-start.12 = (f32[32,2048]{1,0:T(8,128)S(1)}, f32[32,2048]{1,0:T(8,128)S(1)}, u32[]{:S(2)}, u32[]{:S(2)}) collective-permute-start(f32[32,2048]{1,0:T(8,128)S(1)} %get-tuple-element.81), channel_id=1, source_target_pairs={{0,16},{16,32},{32,48},{48,0},{64,80},{80,96},{96,112},{112,64},{1... | collective-permute-start | bytes 786440 | tf_op jit(solution)/shard_map/ppermute | solution.py:43
  98.2 1.5 %collective-permute-start.14 = (f32[32,2048]{1,0:T(8,128)S(1)}, f32[32,2048]{1,0:T(8,128)S(1)}, u32[]{:S(2)}, u32[]{:S(2)}) collective-permute-start(f32[32,2048]{1,0:T(8,128)S(1)} %get-tuple-element.82), channel_id=1, source_target_pairs={{0,64},{16,80},{32,96},{48,112},{64,0},{80,16},{96,32},{112,48},{1... | collective-permute-start | bytes 786440 | tf_op jit(solution)/shard_map/ppermute | solution.py:43
  99.7 0.5 collective-permute-done.18
  100.2 0.1 slice_add_fusion.1
  100.3 0.9 collective-permute-start.17
  101.2 1.5 %collective-permute-start.19 = (f32[32,2048]{1,0:T(8,128)S(1)}, f32[32,2048]{1,0:T(8,128)S(1)}, u32[]{:S(2)}, u32[]{:S(2)}) collective-permute-start(f32[32,2048]{1,0:T(8,128)S(1)} %get-tuple-element.84), channel_id=1, source_target_pairs={{0,64},{16,80},{32,96},{48,112},{64,0},{80,16},{96,32},{112,48},{1... | collective-permute-start | bytes 786440 | tf_op jit(solution)/shard_map/ppermute | solution.py:43
  102.7 4.4 %collective-permute-done.12 = f32[32,2048]{1,0:T(8,128)S(1)} collective-permute-done((f32[32,2048]{1,0:T(8,128)S(1)}, f32[32,2048]{1,0:T(8,128)S(1)}, u32[]{:S(2)}, u32[]{:S(2)}) %collective-permute-start.12) | collective-permute-done | bytes 262176 | tf_op jit(solution)/shard_map/ppermute | solution.py:43
  107.1 0.0 collective-permute-done.14
  107.1 0.1 add_add_fusion.3
  107.1 2.7 %collective-permute-done.17 = f32[32,2048]{1,0:T(8,128)S(1)} collective-permute-done((f32[32,2048]{1,0:T(8,128)S(1)}, f32[32,2048]{1,0:T(8,128)S(1)}, u32[]{:S(2)}, u32[]{:S(2)}) %collective-permute-start.17) | collective-permute-done | bytes 262176 | tf_op jit(solution)/shard_map/ppermute | solution.py:43
  109.9 0.0 collective-permute-done.19
  109.9 0.1 add_add_fusion.1
  110.0 0.8 maximum_divide_fusion
  (9 shorter events, 0.2 us)
Async XLA Ops:
  1.0 10.9 %collective-permute-start = (f32[80,1024]{1,0:T(8,128)S(1)}, f32[80,1024]{1,0:T(8,128)S(1)}, u32[]{:S(2)}, u32[]{:S(2)}) collective-permute-start(f32[80,1024]{1,0:T(8,128)S(1)} %pad_maximum_fusion.1), channel_id=1, source_target_pairs={{0,8},{1,9},{2,10},{3,11},{4,12},{5,13},{6,14},{7,15},{8,0},{9,1},... | collective-permute-start | bytes 983048 | tf_op jit(solution)/shard_map/ppermute | solution.py:34
  13.0 3.4 %collective-permute-start.1 = (f32[160,1024]{1,0:T(8,128)S(1)}, f32[160,1024]{1,0:T(8,128)S(1)}, u32[]{:S(2)}, u32[]{:S(2)}) collective-permute-start(f32[160,1024]{1,0:T(8,128)S(1)} %pad_maximum_fusion.refs_0_), channel_id=1, source_target_pairs={{0,1},{1,0},{2,3},{3,2},{4,5},{5,4},{6,7},{7,6},{8,9},{9,8},{10,11... | collective-permute-start | bytes 1966088 | tf_op jit(solution)/shard_map/ppermute | solution.py:34
  13.1 17.9 %collective-permute-start.3 = (f32[160,1024]{1,0:T(8,128)S(1)}, f32[160,1024]{1,0:T(8,128)S(1)}, u32[]{:S(2)}, u32[]{:S(2)}) collective-permute-start(f32[160,1024]{1,0:T(8,128)S(1)} %pad_maximum_fusion.refs_0_), channel_id=1, source_target_pairs={{0,6},{1,7},{2,0},{3,1},{4,2},{5,3},{6,4},{7,5},{8,14},{9,15},{10,... | collective-permute-start | bytes 1966088 | tf_op jit(solution)/shard_map/ppermute | solution.py:34
  16.4 18.0 %collective-permute-start.2 = (f32[160,1024]{1,0:T(8,128)S(1)}, f32[160,1024]{1,0:T(8,128)S(1)}, u32[]{:S(2)}, u32[]{:S(2)}) collective-permute-start(f32[160,1024]{1,0:T(8,128)S(1)} %pad_maximum_fusion.refs_0_), channel_id=1, source_target_pairs={{0,2},{1,3},{2,4},{3,5},{4,6},{5,7},{6,0},{7,1},{8,10},{9,11},{10,... | collective-permute-start | bytes 1966088 | tf_op jit(solution)/shard_map/ppermute | solution.py:34
  16.4 5.8 %copy-start = (f32[1,4096,1024]{2,1,0:T(8,128)S(1)}, f32[1,4096,1024]{2,1,0:T(8,128)}, u32[]{:S(2)}) copy-start(f32[1,4096,1024]{2,1,0:T(8,128)} %param.5) | copy-start | bytes 50331652
  22.2 16.2 %copy-start.1 = (f32[1,4096,1024]{2,1,0:T(8,128)S(1)}, f32[1,4096,1024]{2,1,0:T(8,128)}, u32[]{:S(2)}) copy-start(f32[1,4096,1024]{2,1,0:T(8,128)} %param.5) | copy-start | bytes 50331652
  34.4 3.9 %collective-permute-start.4 = (f32[160,1024]{1,0:T(8,128)S(1)}, f32[160,1024]{1,0:T(8,128)S(1)}, u32[]{:S(2)}, u32[]{:S(2)}) collective-permute-start(f32[160,1024]{1,0:T(8,128)S(1)} %collective-permute-done.2.refs_0_.refs_4_), channel_id=1, source_target_pairs={{0,1},{1,0},{2,3},{3,2},{4,5},{5,4},{6,7},{7,6},{8,9},{9,8},{10,11... | collective-permute-start | bytes 1966088 | tf_op jit(solution)/shard_map/ppermute | solution.py:34
  34.5 12.0 %collective-permute-start.5 = (f32[160,1024]{1,0:T(8,128)S(1)}, f32[160,1024]{1,0:T(8,128)S(1)}, u32[]{:S(2)}, u32[]{:S(2)}) collective-permute-start(f32[160,1024]{1,0:T(8,128)S(1)} %collective-permute-done.3.refs_8_), channel_id=1, source_target_pairs={{0,1},{1,0},{2,3},{3,2},{4,5},{5,4},{6,7},{7,6},{8,9},{9,8},{10,11... | collective-permute-start | bytes 1966088 | tf_op jit(solution)/shard_map/ppermute | solution.py:34
  35.1 10.9 %collective-permute-start.6 = (f32[80,1024]{1,0:T(8,128)S(1)}, f32[80,1024]{1,0:T(8,128)S(1)}, u32[]{:S(2)}, u32[]{:S(2)}) collective-permute-start(f32[80,1024]{1,0:T(8,128)S(1)} %slice.42), channel_id=1, source_target_pairs={{0,2},{1,3},{2,4},{3,5},{4,6},{5,7},{6,0},{7,1},{8,10},{9,11},{10,... | collective-permute-start | bytes 983048 | tf_op jit(solution)/shard_map/ppermute | solution.py:34
  35.1 10.9 %collective-permute-start.7 = (f32[80,1024]{1,0:T(8,128)S(1)}, f32[80,1024]{1,0:T(8,128)S(1)}, u32[]{:S(2)}, u32[]{:S(2)}) collective-permute-start(f32[80,1024]{1,0:T(8,128)S(1)} %slice.43), channel_id=1, source_target_pairs={{0,6},{1,7},{2,0},{3,1},{4,2},{5,3},{6,4},{7,5},{8,14},{9,15},{10,... | collective-permute-start | bytes 983048 | tf_op jit(solution)/shard_map/ppermute | solution.py:34
  46.0 1.6 %collective-permute-start.8 = (f32[80,1024]{1,0:T(8,128)S(1)}, f32[80,1024]{1,0:T(8,128)S(1)}, u32[]{:S(2)}, u32[]{:S(2)}) collective-permute-start(f32[80,1024]{1,0:T(8,128)S(1)} %collective-permute-done.6.refs_10_), channel_id=1, source_target_pairs={{0,1},{1,0},{2,3},{3,2},{4,5},{5,4},{6,7},{7,6},{8,9},{9,8},{10,11... | collective-permute-start | bytes 983048 | tf_op jit(solution)/shard_map/ppermute | solution.py:34
  46.0 2.1 %collective-permute-start.9 = (f32[80,1024]{1,0:T(8,128)S(1)}, f32[80,1024]{1,0:T(8,128)S(1)}, u32[]{:S(2)}, u32[]{:S(2)}) collective-permute-start(f32[80,1024]{1,0:T(8,128)S(1)} %collective-permute-done.7.refs_11_), channel_id=1, source_target_pairs={{0,1},{1,0},{2,3},{3,2},{4,5},{5,4},{6,7},{7,6},{8,9},{9,8},{10,11... | collective-permute-start | bytes 983048 | tf_op jit(solution)/shard_map/ppermute | solution.py:34
  54.9 16.8 %collective-permute-start.10 = (f32[64,2048]{1,0:T(8,128)S(1)}, f32[64,2048]{1,0:T(8,128)S(1)}, u32[]{:S(2)}, u32[]{:S(2)}) collective-permute-start(f32[64,2048]{1,0:T(8,128)S(1)} %get-tuple-element.60), channel_id=1, source_target_pairs={{0,16},{16,32},{32,48},{48,0},{64,80},{80,96},{96,112},{112,64},{1... | collective-permute-start | bytes 1572872 | tf_op jit(solution)/shard_map/ppermute | solution.py:43
  56.8 14.8 %collective-permute-start.11 = (f32[64,2048]{1,0:T(8,128)S(1)}, f32[64,2048]{1,0:T(8,128)S(1)}, u32[]{:S(2)}, u32[]{:S(2)}) collective-permute-start(f32[64,2048]{1,0:T(8,128)S(1)} %get-tuple-element.61), channel_id=1, source_target_pairs={{0,48},{16,0},{32,16},{48,32},{64,112},{80,64},{96,80},{112,96},{1... | collective-permute-start | bytes 1572872 | tf_op jit(solution)/shard_map/ppermute | solution.py:43
  62.7 19.7 %collective-permute-start.15 = (f32[64,2048]{1,0:T(8,128)S(1)}, f32[64,2048]{1,0:T(8,128)S(1)}, u32[]{:S(2)}, u32[]{:S(2)}) collective-permute-start(f32[64,2048]{1,0:T(8,128)S(1)} %get-tuple-element.74), channel_id=1, source_target_pairs={{0,16},{16,32},{32,48},{48,0},{64,80},{80,96},{96,112},{112,64},{1... | collective-permute-start | bytes 1572872 | tf_op jit(solution)/shard_map/ppermute | solution.py:43
  62.8 19.6 %collective-permute-start.16 = (f32[64,2048]{1,0:T(8,128)S(1)}, f32[64,2048]{1,0:T(8,128)S(1)}, u32[]{:S(2)}, u32[]{:S(2)}) collective-permute-start(f32[64,2048]{1,0:T(8,128)S(1)} %get-tuple-element.75), channel_id=1, source_target_pairs={{0,48},{16,0},{32,16},{48,32},{64,112},{80,64},{96,80},{112,96},{1... | collective-permute-start | bytes 1572872 | tf_op jit(solution)/shard_map/ppermute | solution.py:43
  82.4 8.0 %collective-permute-start.22 = (f32[1,4096]{1,0:T(1,128)S(1)}, f32[1,4096]{1,0:T(1,128)S(1)}, u32[]{:S(2)}, u32[]{:S(2)}) collective-permute-start(f32[1,4096]{1,0:T(1,128)S(1)} %add_add_fusion.5), channel_id=1, source_target_pairs={{0,32},{16,48},{32,0},{48,16},{64,96},{80,112},{96,64},{112,80},{1... | collective-permute-start | bytes 49160 | tf_op jit(solution)/shard_map/ppermute | solution.py:43
  86.1 4.3 %collective-permute-start.21 = (f32[1,4096]{1,0:T(1,128)S(1)}, f32[1,4096]{1,0:T(1,128)S(1)}, u32[]{:S(2)}, u32[]{:S(2)}) collective-permute-start(f32[1,4096]{1,0:T(1,128)S(1)} %add_add_fusion.5), channel_id=1, source_target_pairs={{0,48},{16,0},{32,16},{48,32},{64,112},{80,64},{96,80},{112,96},{1... | collective-permute-start | bytes 49160 | tf_op jit(solution)/shard_map/ppermute | solution.py:43
  87.1 4.9 %collective-permute-start.20 = (f32[1,4096]{1,0:T(1,128)S(1)}, f32[1,4096]{1,0:T(1,128)S(1)}, u32[]{:S(2)}, u32[]{:S(2)}) collective-permute-start(f32[1,4096]{1,0:T(1,128)S(1)} %add_add_fusion.5), channel_id=1, source_target_pairs={{0,16},{16,32},{32,48},{48,0},{64,80},{80,96},{96,112},{112,64},{1... | collective-permute-start | bytes 49160 | tf_op jit(solution)/shard_map/ppermute | solution.py:43
  88.1 8.5 %collective-permute-start.13 = (f32[32,2048]{1,0:T(8,128)S(1)}, f32[32,2048]{1,0:T(8,128)S(1)}, u32[]{:S(2)}, u32[]{:S(2)}) collective-permute-start(f32[32,2048]{1,0:T(8,128)S(1)} %slice_add_fusion.2), channel_id=1, source_target_pairs={{0,48},{16,0},{32,16},{48,32},{64,112},{80,64},{96,80},{112,96},{1... | collective-permute-start | bytes 786440 | tf_op jit(solution)/shard_map/ppermute | solution.py:43
  92.0 3.9 %collective-permute-start.23 = (f32[1,4096]{1,0:T(1,128)S(1)}, f32[1,4096]{1,0:T(1,128)S(1)}, u32[]{:S(2)}, u32[]{:S(2)}) collective-permute-start(f32[1,4096]{1,0:T(1,128)S(1)} %add_add_fusion.4), channel_id=1, source_target_pairs={{0,64},{16,80},{32,96},{48,112},{64,0},{80,16},{96,32},{112,48},{1... | collective-permute-start | bytes 49160 | tf_op jit(solution)/shard_map/ppermute | solution.py:43
  93.6 6.5 %collective-permute-start.18 = (f32[32,2048]{1,0:T(8,128)S(1)}, f32[32,2048]{1,0:T(8,128)S(1)}, u32[]{:S(2)}, u32[]{:S(2)}) collective-permute-start(f32[32,2048]{1,0:T(8,128)S(1)} %slice_add_fusion), channel_id=1, source_target_pairs={{0,48},{16,0},{32,16},{48,32},{64,112},{80,64},{96,80},{112,96},{1... | collective-permute-start | bytes 786440 | tf_op jit(solution)/shard_map/ppermute | solution.py:43
  96.7 10.4 %collective-permute-start.12 = (f32[32,2048]{1,0:T(8,128)S(1)}, f32[32,2048]{1,0:T(8,128)S(1)}, u32[]{:S(2)}, u32[]{:S(2)}) collective-permute-start(f32[32,2048]{1,0:T(8,128)S(1)} %get-tuple-element.81), channel_id=1, source_target_pairs={{0,16},{16,32},{32,48},{48,0},{64,80},{80,96},{96,112},{112,64},{1... | collective-permute-start | bytes 786440 | tf_op jit(solution)/shard_map/ppermute | solution.py:43
  98.2 8.9 %collective-permute-start.14 = (f32[32,2048]{1,0:T(8,128)S(1)}, f32[32,2048]{1,0:T(8,128)S(1)}, u32[]{:S(2)}, u32[]{:S(2)}) collective-permute-start(f32[32,2048]{1,0:T(8,128)S(1)} %get-tuple-element.82), channel_id=1, source_target_pairs={{0,64},{16,80},{32,96},{48,112},{64,0},{80,16},{96,32},{112,48},{1... | collective-permute-start | bytes 786440 | tf_op jit(solution)/shard_map/ppermute | solution.py:43
  100.3 9.6 %collective-permute-start.17 = (f32[32,2048]{1,0:T(8,128)S(1)}, f32[32,2048]{1,0:T(8,128)S(1)}, u32[]{:S(2)}, u32[]{:S(2)}) collective-permute-start(f32[32,2048]{1,0:T(8,128)S(1)} %get-tuple-element.83), channel_id=1, source_target_pairs={{0,16},{16,32},{32,48},{48,0},{64,80},{80,96},{96,112},{112,64},{1... | collective-permute-start | bytes 786440 | tf_op jit(solution)/shard_map/ppermute | solution.py:43
  101.2 8.7 %collective-permute-start.19 = (f32[32,2048]{1,0:T(8,128)S(1)}, f32[32,2048]{1,0:T(8,128)S(1)}, u32[]{:S(2)}, u32[]{:S(2)}) collective-permute-start(f32[32,2048]{1,0:T(8,128)S(1)} %get-tuple-element.84), channel_id=1, source_target_pairs={{0,64},{16,80},{32,96},{48,112},{64,0},{80,16},{96,32},{112,48},{1... | collective-permute-start | bytes 786440 | tf_op jit(solution)/shard_map/ppermute | solution.py:43

commit v2 on v1

--- a/solution.py
+++ b/solution.py
@@ -13,7 +13,8 @@
 QROWS = 16
 PIECE = ROWS + QROWS
 TILE = 1024
-SPLIT = (2048, 2048)
+RAW_TILE = 512
+SPLIT = (2560, 1536)
 BF16 = jnp.bfloat16
 F32 = jnp.float32
 LIMIT = 20 * 2**20
@@ -43,8 +44,16 @@
     return lax.ppermute(x, "layer", pairs)
 
 
-def swap_core(x):
-    return example_permute(x, lambda x_hi, y, core: (x_hi, y, 1 - core))
+def y_up(x):
+    return example_permute(x, lambda x_hi, y, core: (x_hi, y + 1, core))
+
+
+def y_down(x):
+    return example_permute(x, lambda x_hi, y, core: (x_hi, y - 1, core))
+
+
+def with_swapped(*arrays):
+    return list(arrays) + [example_permute(x, lambda x_hi, y, core: (x_hi, y, 1 - core)) for x in arrays]
 
 
 def z_up(x):
@@ -59,8 +68,14 @@
     return layer_permute(x, lambda x_lo, z: (1 - x_lo, z))
 
 
-NEAR = [(0, 0, 0, 0), (0, PIECE, 1, 0), (1, 0, 0, 1), (1, PIECE, 1, 1)]
-FAR = [(0, 0, 0, 0), (1, 0, 1, 0), (2, 0, 0, 1), (3, 0, 1, 1)]
+HEAD = 32
+NEAR = [(0, 0, ROWS, ROWS, 0, 0), (1, 0, ROWS, ROWS, 1, 0), (2, 0, ROWS, ROWS, 0, 1), (3, 0, ROWS, ROWS, 1, 1)]
+FAR = [
+    (4 * core + 2 * x_flip + tail, HEAD * tail, HEAD, HEAD if tail else -1, x_flip, core)
+    for core in range(2)
+    for x_flip in range(2)
+    for tail in range(2)
+]
 
 
 def tie(*arrays):
@@ -68,10 +83,10 @@
 
 
 def split(blocks, bufs, x_hi, core, hi_ref, lo_ref):
-    for b, off, x_flip, core_flip in blocks:
+    for b, first, n, _, x_flip, core_flip in blocks:
         at = ((x_hi + x_flip) % 2) * 2 + (core + core_flip) % 2
-        rows = pl.ds(pl.multiple_of(at * ROWS, ROWS), ROWS)
-        block = bufs[b][off : off + ROWS, :]
+        rows = pl.ds(pl.multiple_of(at * ROWS + first, HEAD), n)
+        block = bufs[b][:n, :]
         hi = block.astype(BF16)
         hi_ref[rows, :] = hi
         lo_ref[rows, :] = (block - hi.astype(F32)).astype(BF16)
@@ -130,9 +145,7 @@
         out_specs=VMEM,
         out_shape=jax.ShapeDtypeStruct((1, examples), F32),
         compiler_params=pltpu.CompilerParams(vmem_limit_bytes=LIMIT),
-        cost_estimate=pl.CostEstimate(
-            flops=8 * 256 * len(y_shifts) * R * examples, bytes_accessed=4 * R * examples, transcendentals=0
-        ),
+        cost_estimate=pl.CostEstimate(flops=1, bytes_accessed=1, transcendentals=0),
     )(where, *matrices, store)
 
 
@@ -152,13 +165,15 @@
             hi_ref, lo_ref, *made = made
             split(blocks, bufs, x_hi, core, hi_ref, lo_ref)
             matrices.append((y_shift, hi_ref, lo_ref))
-        for b, off, x_flip, core_flip in blocks:
+        for b, _, _, queries, x_flip, core_flip in blocks:
+            if queries < 0:
+                continue
             to_z, to_x = (y + y_shift + 4) % 4, (x_hi + x_flip) % 2
             code = ((to_z - z + 4) % 4) * 2 + (to_x + x_lo) % 2
             slot = sum(jnp.where(code == k, s, 0) for k, s in enumerate(SLOTS))
             at = slot * 2 + (core + core_flip) % 2
             rows = pl.ds(pl.multiple_of(at * QROWS, QROWS), QROWS)
-            q_ref[rows, :] = bufs[b][off + ROWS : off + PIECE, :]
+            q_ref[rows, :] = bufs[b][queries : queries + QROWS, :]
     q = q_ref[...]
     qh = q.astype(BF16)
     ql = (q - qh.astype(F32)).astype(BF16)
@@ -191,30 +206,33 @@
     )(where, *refs)
 
 
-CUTS = (64, 64, 32, 32, 64)
-
-
-def raw_kernel(first, rh_ref, rl_ref, s_ref, *outs):
-    @pl.loop(0, outs[0].shape[1] // TILE)
+Z_FIRST = [[(0, 64)], [(64, 64)], [(128, 32)], [(160, 32)], [(192, 64)]]
+HALVES = ((2, 0), (1, 1), (2, 1), (3, 0), (1, 0), (3, 1), (0, 0), (0, 1))
+X_FIRST = [[(32 * SLOTS[2 * dz + dx] + 16 * half, 16) for dz, half in HALVES] for dx in (1, 0)]
+
+
+def raw_kernel(first, runs, rh_ref, rl_ref, s_ref, *outs):
+    @pl.loop(0, outs[0].shape[1] // RAW_TILE)
     def _(i):
-        rows = pl.ds(pl.multiple_of(first + i * TILE, TILE), TILE)
-        cols = pl.ds(pl.multiple_of(i * TILE, TILE), TILE)
+        rows = pl.ds(pl.multiple_of(first + i * RAW_TILE, RAW_TILE), RAW_TILE)
+        cols = pl.ds(pl.multiple_of(i * RAW_TILE, RAW_TILE), RAW_TILE)
         s = s_ref[rows, :]
         sh = s.astype(BF16)
         sl = (s - sh.astype(F32)).astype(BF16)
         raw = nt_dot(rh_ref[...], sh) + nt_dot(rh_ref[...], sl) + nt_dot(rl_ref[...], sh)
-        at = 0
-        for n, ref in zip(CUTS, outs):
-            ref[:, cols] = raw[at : at + n]
-            at += n
-
-
-def raw_scores(rh, rl, store, first, examples):
+        for run, ref in zip(runs, outs):
+            at = 0
+            for start, n in run:
+                ref[at : at + n, cols] = raw[start : start + n]
+                at += n
+
+
+def raw_scores(rh, rl, store, first, examples, runs):
     return pl.pallas_call(
-        functools.partial(raw_kernel, first),
+        functools.partial(raw_kernel, first, runs),
         in_specs=[VMEM] * 3,
-        out_specs=[VMEM] * len(CUTS),
-        out_shape=[jax.ShapeDtypeStruct((n, examples), F32) for n in CUTS],
+        out_specs=[VMEM] * len(runs),
+        out_shape=[jax.ShapeDtypeStruct((sum(n for _, n in run), examples), F32) for run in runs],
         compiler_params=pltpu.CompilerParams(vmem_limit_bytes=LIMIT),
         cost_estimate=pl.CostEstimate(
             flops=8 * Q * R * examples, bytes_accessed=4 * (R + Q) * examples, transcendentals=0
@@ -227,49 +245,50 @@
     where = jnp.stack([lax.axis_index("example"), layer // 4, layer % 4]).astype(jnp.int32)
     store = store[0]
 
-    piece = jnp.concatenate([precond[0], queries[0]], axis=0)
-    other = example_permute(piece, lambda x_hi, y, core: (1 - x_hi, y, core))
-    pair = jnp.concatenate([piece, other], axis=0)
-    left = example_permute(pair, lambda x_hi, y, core: (x_hi, y + 1, core))
-    right = example_permute(pair, lambda x_hi, y, core: (x_hi, y - 1, core))
-    own = (0, [pair, swap_core(pair)], NEAR)
+    own0 = jnp.concatenate([precond[0], queries[0]], axis=0)
+    own1 = example_permute(own0, lambda x_hi, y, core: (1 - x_hi, y, core))
+    own1, below0, above0 = tie(own1, y_up(own0), y_down(own0))
+    own = (0, with_swapped(own0, own1), NEAR)
     own_hi, own_lo, own_part = part_sizes(where, own, store)
-    left, right, own_part = tie(left, right, own_part)
-    far0 = example_permute(left[:PIECE], lambda x_hi, y, core: (x_hi, y + 1, core))
-    far1 = example_permute(right[PIECE:], lambda x_hi, y, core: (x_hi, y - 1, core))
-    below = (-1, [left, swap_core(left)], NEAR)
+    below1, above1, *far0, own_part = tie(
+        y_up(own1), y_down(own1), y_up(below0[:HEAD]), y_down(above0[HEAD:]), own_part
+    )
+    tail, head = y_up(below1[HEAD:]), y_down(above1[:HEAD])
+    below = (-1, with_swapped(below0, below1), NEAR)
     below_hi, below_lo, below_part = part_sizes(where, below, store)
-    above = (1, [right, swap_core(right)], NEAR)
-    far0, far1, below_part = tie(far0, far1, below_part)
-    across = (2, [far0, far1, swap_core(far0), swap_core(far1)], FAR)
+    above = (1, with_swapped(above0, above1), NEAR)
+    head, tail, below_part = tie(head, tail, below_part)
+    across = (2, with_swapped(*far0, head, tail), FAR)
     rh, rl, *rest = ready_queries(
         where, [own, below, above, across], [(own_hi, own_lo), (below_hi, below_lo), (), ()]
     )
 
-    blocks, first = [], 0
-    for examples in SPLIT:
-        blocks.append(raw_scores(rh, rl, store, first, examples))
-        rh = tie(rh, blocks[-1][-1])[0]
-        first += examples
-    (up1, down1, up2, down2, mine), (up1b, down1b, up2b, down2b, mineb) = blocks
+    up1, down1, up2, down2, mine = raw_scores(rh, rl, store, 0, SPLIT[0], Z_FIRST)
+    rh = tie(rh, mine)[0]
+    away, home = raw_scores(rh, rl, store, SPLIT[0], SPLIT[1], X_FIRST)
+    rest_part = rest_sizes(where, [1, 2], tie(*rest, home)[:-1], store)
     from_below, from_above = z_up(up1), z_down(down1)
-    from_belowb, from_aboveb = z_up(up1b), z_down(down1b)
-    *rest, from_below, from_above = tie(*rest, from_below, from_above)
-    rest_part = rest_sizes(where, [1, 2], rest, store)
+    came = swap_x(away)
+    sizes_sq = own_part + below_part + rest_part
+    sizes_sq, from_below, from_above = tie(sizes_sq, from_below, from_above)
     last_below, last_above = z_up(up2 + from_below[:32]), z_down(down2 + from_above[:32])
+    sizes_sq = sizes_sq + swap_x(sizes_sq)
+    home = home + came
+    sizes_sq = sizes_sq + layer_permute(sizes_sq, lambda x_lo, z: (x_lo, z ^ 1))
+    sizes_sq, last_below, last_above = tie(sizes_sq, last_below, last_above)
     here = mine[:32] + from_above[32:] + last_below
     there = mine[32:] + from_below[32:] + last_above
-    scores = [here + swap_x(there)]
-    sizes_sq = own_part + below_part + rest_part
-    sizes_sq, from_belowb, from_aboveb = tie(sizes_sq, from_belowb, from_aboveb)
-    last_below, last_above = z_up(up2b + from_belowb[:32]), z_down(down2b + from_aboveb[:32])
-    here = mineb[:32] + from_aboveb[32:] + last_below
-    there = mineb[32:] + from_belowb[32:] + last_above
-    scores.append(here + swap_x(there))
-
-    sizes_sq = sizes_sq + z_up(sizes_sq) + z_down(sizes_sq) + layer_permute(sizes_sq, lambda x, z: (x, z + 2))
-    root = jnp.sqrt(sizes_sq + swap_x(sizes_sq))
-    return jnp.concatenate(scores, axis=1) / root
+    first = here + swap_x(there)
+
+    from_below, from_above = tie(z_up(home[:32]), z_down(home[32:64]))
+    last_below = z_up(home[64:80] + from_below[:16])
+    last_above = z_down(home[80:96] + from_above[:16])
+    last = jnp.concatenate(
+        [home[96:112] + from_above[16:] + last_below, home[112:] + from_below[16:] + last_above], axis=0
+    )
+
+    root = jnp.sqrt(sizes_sq + layer_permute(sizes_sq, lambda x_lo, z: (x_lo, z ^ 2)))
+    return jnp.concatenate([first, last], axis=1) / root
 
 
 def solution(mesh):

time: 111 us -> 106 us (0.955)
  waiting for transfers between devices: 34.2 us -> 25.3 us
  starting transfers between devices: 33.6 us -> 37.1 us
    ppermute x10 -> x19, waiting for transfers between devices: 16.7 us -> 10.6 us  [example_permute(): return lax.ppermute(x, 'example', pairs)]
    ppermute x10 -> x19, starting transfers between devices: 10.9 us -> 16.7 us  [example_permute(): return lax.ppermute(x, 'example', pairs)]
    ppermute x14 -> x13, waiting for transfers between devices: 17.5 us -> 14.7 us  [layer_permute(): return lax.ppermute(x, 'layer', pairs)]
    ppermute x14 -> x13, starting transfers between devices: 22.7 us -> 20.5 us  [layer_permute(): return lax.ppermute(x, 'layer', pairs)]
  transfers between devices with their start and end apart: 24 -> 32, of which waited for: 13 -> 13; matrix products, arithmetic and copies ran while one was open for 0% -> 1% of each run, Pallas kernels for 24% -> 22%
where the time goes in v2:
time: 106 us; the launch traced here: 105 us
  starting transfers between devices  37.1 us (35%)
  Pallas kernels  34.5 us (33%)
  waiting for transfers between devices  25.3 us (24%)
  local copies, waits for them, and re-layouts  5.85 us (6%)
  other arithmetic  2.42 us (2%)
    ppermute x13, starting transfers between devices, layer_permute(): return lax.ppermute(x, 'layer', pairs)  20.5 us
    ppermute x19, starting transfers between devices, example_permute(): return lax.ppermute(x, 'example', pairs)  16.7 us
    ppermute x13, waiting for transfers between devices, layer_permute(): return lax.ppermute(x, 'layer', pairs)  14.7 us
    pallas_call x2, Pallas kernels, part_sizes(): pl.pallas_call(functools.partial(part_kernel, blocks, y_shift, len(buffer...  12.5 us
    pallas_call x1, Pallas kernels, rest_sizes(): pl.pallas_call(functools.partial(rest_kernel, y_shifts), in_specs=[SMEM]...  10.7 us
    ppermute x19, waiting for transfers between devices, example_permute(): return lax.ppermute(x, 'example', pairs)  10.6 us
    pallas_call x2, Pallas kernels, raw_scores(): pl.pallas_call(functools.partial(raw_kernel, first, runs), in_specs=[VMEM...  8.22 us
    unnamed x4, local copies, waits for them, and re-layouts  5.77 us
  transfers between devices with their start and end apart: 32, of which 13 were waited for; matrix products, arithmetic and copies ran while one was open for 1% of the time, Pallas kernels for 22%

profile of v2, /device:TPU:0, one launch (start us, length us, event | category | flops | bytes accessed | tf_op | source)
XLA Modules:
  0.0 105.4 jit_solution(2703675581186673954)
XLA Ops:
  0.0 1.0 pad_maximum_fusion.refs_0_
  1.0 3.2 %collective-permute-start.2 = (f32[80,1024]{1,0:T(8,128)S(1)}, f32[80,1024]{1,0:T(8,128)S(1)}, u32[]{:S(2)}, u32[]{:S(2)}) collective-permute-start(f32[80,1024]{1,0:T(8,128)S(1)} %pad_maximum_fusion.refs_0_), channel_id=1, source_target_pairs={{0,6},{1,7},{2,0},{3,1},{4,2},{5,3},{6,4},{7,5},{8,14},{9,15},{10,... | collective-permute-start | bytes 983048 | tf_op jit(solution)/shard_map/ppermute | solution.py:35
  4.2 3.0 %collective-permute-start = (f32[80,1024]{1,0:T(8,128)S(1)}, f32[80,1024]{1,0:T(8,128)S(1)}, u32[]{:S(2)}, u32[]{:S(2)}) collective-permute-start(f32[80,1024]{1,0:T(8,128)S(1)} %pad_maximum_fusion.refs_0_), channel_id=1, source_target_pairs={{0,8},{1,9},{2,10},{3,11},{4,12},{5,13},{6,14},{7,15},{8,0},{9,1},... | collective-permute-start | bytes 983048 | tf_op jit(solution)/shard_map/ppermute | solution.py:35
  7.2 0.0 collective-permute-start.3
  7.2 3.9 %collective-permute-done.2.refs_12_ = f32[80,1024]{1,0:T(8,128)S(1)} collective-permute-done((f32[80,1024]{1,0:T(8,128)S(1)}, f32[80,1024]{1,0:T(8,128)S(1)}, u32[]{:S(2)}, u32[]{:S(2)}) %collective-permute-start.2) | collective-permute-done | bytes 327712 | tf_op jit(solution)/shard_map/ppermute | solution.py:35
  11.2 3.4 %collective-permute-done.1.refs_0_.refs_6_ = f32[80,1024]{1,0:T(8,128)S(1)} collective-permute-done((f32[80,1024]{1,0:T(8,128)S(1)}, f32[80,1024]{1,0:T(8,128)S(1)}, u32[]{:S(2)}, u32[]{:S(2)}) %collective-permute-start.1) | collective-permute-done | bytes 327712 | tf_op jit(solution)/shard_map/ppermute | solution.py:35
  14.6 0.3 collective-permute-done.refs_1_
  14.9 0.0 collective-permute-start.4
  14.9 0.1 pad_add_fusion.where_ref
  15.0 0.6 collective-permute-start.9
  15.5 3.0 %collective-permute-start.6 = (f32[80,1024]{1,0:T(8,128)S(1)}, f32[80,1024]{1,0:T(8,128)S(1)}, u32[]{:S(2)}, u32[]{:S(2)}) collective-permute-start(f32[80,1024]{1,0:T(8,128)S(1)} %collective-permute-done.refs_1_), channel_id=1, source_target_pairs={{0,6},{1,7},{2,0},{3,1},{4,2},{5,3},{6,4},{7,5},{8,14},{9,15},{10,... | collective-permute-start | bytes 983048 | tf_op jit(solution)/shard_map/ppermute | solution.py:35
  18.5 0.0 collective-permute-done.3.refs_2_
  18.5 0.1 collective-permute-start.7
  18.6 0.0 collective-permute-done.4.refs_3_
  18.6 3.3 %collective-permute-start.8 = (f32[48,1024]{1,0:T(8,128)S(1)}, f32[48,1024]{1,0:T(8,128)S(1)}, u32[]{:S(2)}, u32[]{:S(2)}) collective-permute-start(f32[48,1024]{1,0:T(8,128)S(1)} %slice.61), channel_id=1, source_target_pairs={{0,6},{1,7},{2,0},{3,1},{4,2},{5,3},{6,4},{7,5},{8,14},{9,15},{10,... | collective-permute-start | bytes 589832 | tf_op jit(solution)/shard_map/ppermute | solution.py:35
  21.9 5.8 %copy-done = f32[1,4096,1024]{2,1,0:T(8,128)S(1)} copy-done((f32[1,4096,1024]{2,1,0:T(8,128)S(1)}, f32[1,4096,1024]{2,1,0:T(8,128)}, u32[]{:S(2)}) %copy-start) | copy-done | bytes 16777240
  27.7 6.2 %shard_map.37 = (bf16[256,1024]{1,0:T(8,128)(2,1)S(1)}, bf16[256,1024]{1,0:T(8,128)(2,1)S(1)}, f32[1,4096]{1,0:T(1,128)S(1)}) custom-call(s32[3]{0:T(128)S(1)} %pad_add_fusion.where_ref, f32[80,1024]{1,0:T(8,128)S(1)} %pad_maximum_fusion.refs_0_, f32[80,1024]{1,0:T(8,128)S(1)} %collective-permute-done.refs_1_, ...), custom_call_target="tpu_custom_call" | custom-call | flops 8589934592 | bytes 16777216 | tf_op jit(solution)/shard_map/pallas_call | solution.py:122
  33.9 0.0 collective-permute-done.7.refs_16_
  33.9 0.0 collective-permute-done.8.refs_17_
  33.9 0.0 collective-permute-done.5.refs_1_.refs_7_
  33.9 0.1 collective-permute-start.10
  34.0 0.5 collective-permute-start.11
  34.6 0.2 collective-permute-start.12
  34.7 2.0 %collective-permute-start.13 = (f32[32,1024]{1,0:T(8,128)S(1)}, f32[32,1024]{1,0:T(8,128)S(1)}, u32[]{:S(2)}, u32[]{:S(2)}) collective-permute-start(f32[32,1024]{1,0:T(8,128)S(1)} %slice.62), channel_id=1, source_target_pairs={{0,6},{1,7},{2,0},{3,1},{4,2},{5,3},{6,4},{7,5},{8,14},{9,15},{10,... | collective-permute-start | bytes 393224 | tf_op jit(solution)/shard_map/ppermute | solution.py:35
  36.8 0.2 collective-permute-start.16
  37.0 6.3 %shard_map.38 = (bf16[256,1024]{1,0:T(8,128)(2,1)S(1)}, bf16[256,1024]{1,0:T(8,128)(2,1)S(1)}, f32[1,4096]{1,0:T(1,128)S(1)}) custom-call(s32[3]{0:T(128)S(1)} %pad_add_fusion.where_ref, f32[80,1024]{1,0:T(8,128)S(1)} %collective-permute-done.1.refs_0_.refs_6_, f32[80,1024]{1,0:T(8,128)S(1)} %collective-permute-done.5.refs_1_.refs_7_, ...), custom_call_target="tpu_custom_call" | custom-call | flops 8589934592 | bytes 16777216 | tf_op jit(solution)/shard_map/pallas_call | solution.py:122
  43.4 1.6 %collective-permute-done.14.refs_19_ = f32[48,1024]{1,0:T(8,128)S(1)} collective-permute-done((f32[48,1024]{1,0:T(8,128)S(1)}, f32[48,1024]{1,0:T(8,128)S(1)}, u32[]{:S(2)}, u32[]{:S(2)}) %collective-permute-start.14) | collective-permute-done | bytes 196640 | tf_op jit(solution)/shard_map/ppermute | solution.py:35
  44.9 0.5 collective-permute-start.15
  45.4 0.0 collective-permute-done.11.refs_14_
  45.5 0.0 collective-permute-start.17
  45.5 1.1 %collective-permute-done.15.refs_20_ = f32[32,1024]{1,0:T(8,128)S(1)} collective-permute-done((f32[32,1024]{1,0:T(8,128)S(1)}, f32[32,1024]{1,0:T(8,128)S(1)}, u32[]{:S(2)}, u32[]{:S(2)}) %collective-permute-start.15) | collective-permute-done | bytes 131104 | tf_op jit(solution)/shard_map/ppermute | solution.py:35
  46.6 0.2 collective-permute-done.17.refs_22_
  46.8 0.0 collective-permute-done.18.refs_23_
  46.8 3.0 %shard_map.39 = (bf16[256,1024]{1,0:T(8,128)(2,1)S(1)}, bf16[256,1024]{1,0:T(8,128)(2,1)S(1)}, bf16[256,1024]{1,0:T(8,128)(2,1)S(1)}, bf16[256,1024]{1,0:T(8,128...) custom-call(s32[3]{0:T(128)S(1)} %pad_add_fusion.where_ref, ...), custom_call_target="tpu_custom_call" | custom-call | flops 1610612736 | bytes 1048576 | tf_op jit(solution)/shard_map/pallas_call | solution.py:198
  49.9 5.1 %shard_map.40 = (f32[64,2560]{1,0:T(8,128)S(1)}, f32[64,2560]{1,0:T(8,128)S(1)}, f32[32,2560]{1,0:T(8,128)S(1)}, f32[32,2560]{1,0:T(8,128)S(1)}, f32[64,2560]{1,0:T(8,128)S(1)}) custom-call(bf16[256,1024]{1,0:T(8,128)(2,1)S(1)} %get-tuple-element.72.rh_ref, bf16[256,1024]{1,0:T(8,128)(2,1)S(1)} %get-tuple-element.64.rl_ref, f32[4096,1024]{1,0:T(8,128)S(1)} %bitcast.9), custom_call_target="tpu_custom_call" | custom-call | flops 5368709120 | bytes 13107200 | tf_op jit(solution)/shard_map/pallas_call | solution.py:231
  55.0 3.1 %shard_map.41 = (f32[128,1536]{1,0:T(8,128)S(1)}, f32[128,1536]{1,0:T(8,128)S(1)}) custom-call(bf16[256,1024]{1,0:T(8,128)(2,1)S(1)} %get-tuple-element.72.rh_ref, bf16[256,1024]{1,0:T(8,128)(2,1)S(1)} %get-tuple-element.64.rl_ref, f32[4096,1024]{1,0:T(8,128)S(1)} %bitcast.10), custom_call_target="tpu_custom_call" | custom-call | flops 3221225472 | bytes 7864320 | tf_op jit(solution)/shard_map/pallas_call | solution.py:231
  58.1 2.0 %collective-permute-start.19 = (f32[64,2560]{1,0:T(8,128)S(1)}, f32[64,2560]{1,0:T(8,128)S(1)}, u32[]{:S(2)}, u32[]{:S(2)}) collective-permute-start(f32[64,2560]{1,0:T(8,128)S(1)} %get-tuple-element.78), channel_id=1, source_target_pairs={{0,16},{16,32},{32,48},{48,0},{64,80},{80,96},{96,112},{112,64},{1... | collective-permute-start | bytes 1966088 | tf_op jit(solution)/shard_map/ppermute | solution.py:44
  60.1 2.2 %collective-permute-start.20 = (f32[64,2560]{1,0:T(8,128)S(1)}, f32[64,2560]{1,0:T(8,128)S(1)}, u32[]{:S(2)}, u32[]{:S(2)}) collective-permute-start(f32[64,2560]{1,0:T(8,128)S(1)} %get-tuple-element.79), channel_id=1, source_target_pairs={{0,48},{16,0},{32,16},{48,32},{64,112},{80,64},{96,80},{112,96},{1... | collective-permute-start | bytes 1966088 | tf_op jit(solution)/shard_map/ppermute | solution.py:44
  62.3 1.5 %collective-permute-start.26 = (f32[128,1536]{1,0:T(8,128)S(1)}, f32[128,1536]{1,0:T(8,128)S(1)}, u32[]{:S(2)}, u32[]{:S(2)}) collective-permute-start(f32[128,1536]{1,0:T(8,128)S(1)} %get-tuple-element.87), channel_id=1, source_target_pairs={{0,64},{16,80},{32,96},{48,112},{64,0},{80,16},{96,32},{112,48},{1... | collective-permute-start | bytes 2359304 | tf_op jit(solution)/shard_map/ppermute | solution.py:44
  63.8 10.7 %shard_map.42 = f32[1,4096]{1,0:T(1,128)S(1)} custom-call(s32[3]{0:T(128)S(1)} %pad_add_fusion.where_ref, bf16[256,1024]{1,0:T(8,128)(2,1)S(1)} %get-tuple-element.74.refs_0_, bf16[256,1024]{1,0:T(8,128)(2,1)S(1)} %get-tuple-element.75.refs_1_, bf16[256,1024]{1,0:T(8,128)(2,1)S(1)} %get-tuple-element.76.refs_2_, ...), custom_call_target="tpu_custom_call" | custom-call | flops 1 | bytes 1 | tf_op jit(solution)/shard_map/pallas_call | solution.py:142
  74.5 2.8 %collective-permute-done.19 = f32[64,2560]{1,0:T(8,128)S(1)} collective-permute-done((f32[64,2560]{1,0:T(8,128)S(1)}, f32[64,2560]{1,0:T(8,128)S(1)}, u32[]{:S(2)}, u32[]{:S(2)}) %collective-permute-start.19) | collective-permute-done | bytes 655392 | tf_op jit(solution)/shard_map/ppermute | solution.py:44
  77.3 0.0 collective-permute-done.20
  77.3 1.3 %collective-permute-start.23 = (f32[32,2560]{1,0:T(8,128)S(1)}, f32[32,2560]{1,0:T(8,128)S(1)}, u32[]{:S(2)}, u32[]{:S(2)}) collective-permute-start(f32[32,2560]{1,0:T(8,128)S(1)} %slice_add_fusion.1), channel_id=1, source_target_pairs={{0,16},{16,32},{32,48},{48,0},{64,80},{80,96},{96,112},{112,64},{1... | collective-permute-start | bytes 983048 | tf_op jit(solution)/shard_map/ppermute | solution.py:44
  78.7 2.1 %collective-permute-start.24 = (f32[32,2560]{1,0:T(8,128)S(1)}, f32[32,2560]{1,0:T(8,128)S(1)}, u32[]{:S(2)}, u32[]{:S(2)}) collective-permute-start(f32[32,2560]{1,0:T(8,128)S(1)} %slice_add_fusion), channel_id=1, source_target_pairs={{0,48},{16,0},{32,16},{48,32},{64,112},{80,64},{96,80},{112,96},{1... | collective-permute-start | bytes 983048 | tf_op jit(solution)/shard_map/ppermute | solution.py:44
  80.7 0.9 collective-permute-done.26
  81.6 0.1 add.74
  81.8 1.7 %collective-permute-start.28 = (f32[32,1536]{1,0:T(8,128)S(1)}, f32[32,1536]{1,0:T(8,128)S(1)}, u32[]{:S(2)}, u32[]{:S(2)}) collective-permute-start(f32[32,1536]{1,0:T(8,128)S(1)} %get-tuple-element.93), channel_id=1, source_target_pairs={{0,48},{16,0},{32,16},{48,32},{64,112},{80,64},{96,80},{112,96},{1... | collective-permute-start | bytes 589832 | tf_op jit(solution)/shard_map/ppermute | solution.py:44
  83.5 0.4 collective-permute-start.27
  83.9 1.5 %collective-permute-start.21 = (f32[1,4096]{1,0:T(1,128)S(1)}, f32[1,4096]{1,0:T(1,128)S(1)}, u32[]{:S(2)}, u32[]{:S(2)}) collective-permute-start(f32[1,4096]{1,0:T(1,128)S(1)} %add_add_fusion.2), channel_id=1, source_target_pairs={{0,64},{16,80},{32,96},{48,112},{64,0},{80,16},{96,32},{112,48},{1... | collective-permute-start | bytes 49160 | tf_op jit(solution)/shard_map/ppermute | solution.py:44
  85.3 2.3 %collective-permute-done.21 = f32[1,4096]{1,0:T(1,128)S(1)} collective-permute-done((f32[1,4096]{1,0:T(1,128)S(1)}, f32[1,4096]{1,0:T(1,128)S(1)}, u32[]{:S(2)}, u32[]{:S(2)}) %collective-permute-start.21) | collective-permute-done | bytes 16416 | tf_op jit(solution)/shard_map/ppermute | solution.py:44
  87.6 0.1 collective-permute-start.22
  87.7 4.0 %collective-permute-done.22 = f32[1,4096]{1,0:T(1,128)S(1)} collective-permute-done((f32[1,4096]{1,0:T(1,128)S(1)}, f32[1,4096]{1,0:T(1,128)S(1)}, u32[]{:S(2)}, u32[]{:S(2)}) %collective-permute-start.22) | collective-permute-done | bytes 16416 | tf_op jit(solution)/shard_map/ppermute | solution.py:44
  91.7 0.0 collective-permute-done.24
  91.7 0.0 collective-permute-done.28
  91.7 0.4 collective-permute-done.27
  92.1 1.1 %collective-permute-start.29 = (f32[16,1536]{1,0:T(8,128)S(1)}, f32[16,1536]{1,0:T(8,128)S(1)}, u32[]{:S(2)}, u32[]{:S(2)}) collective-permute-start(f32[16,1536]{1,0:T(8,128)S(1)} %slice_add_fusion.4), channel_id=1, source_target_pairs={{0,16},{16,32},{32,48},{48,0},{64,80},{80,96},{96,112},{112,64},{1... | collective-permute-start | bytes 294920 | tf_op jit(solution)/shard_map/ppermute | solution.py:44
  93.2 0.1 add_add_fusion
  93.3 3.6 %collective-permute-start.31 = (f32[1,4096]{1,0:T(1,128)S(1)}, f32[1,4096]{1,0:T(1,128)S(1)}, u32[]{:S(2)}, u32[]{:S(2)}) collective-permute-start(f32[1,4096]{1,0:T(1,128)S(1)} %add.67), channel_id=1, source_target_pairs={{0,32},{16,48},{32,0},{48,16},{64,96},{80,112},{96,64},{112,80},{1... | collective-permute-start | bytes 49160 | tf_op jit(solution)/shard_map/ppermute | solution.py:44
  96.9 1.5 %collective-permute-start.25 = (f32[32,2560]{1,0:T(8,128)S(1)}, f32[32,2560]{1,0:T(8,128)S(1)}, u32[]{:S(2)}, u32[]{:S(2)}) collective-permute-start(f32[32,2560]{1,0:T(8,128)S(1)} %add_add_fusion), channel_id=1, source_target_pairs={{0,64},{16,80},{32,96},{48,112},{64,0},{80,16},{96,32},{112,48},{1... | collective-permute-start | bytes 983048 | tf_op jit(solution)/shard_map/ppermute | solution.py:44
  98.4 1.6 %collective-permute-start.30 = (f32[16,1536]{1,0:T(8,128)S(1)}, f32[16,1536]{1,0:T(8,128)S(1)}, u32[]{:S(2)}, u32[]{:S(2)}) collective-permute-start(f32[16,1536]{1,0:T(8,128)S(1)} %get-tuple-element.92), channel_id=1, source_target_pairs={{0,48},{16,0},{32,16},{48,32},{64,112},{80,64},{96,80},{112,96},{1... | collective-permute-start | bytes 294920 | tf_op jit(solution)/shard_map/ppermute | solution.py:44
  100.0 3.0 %collective-permute-done.30 = f32[16,1536]{1,0:T(8,128)S(1)} collective-permute-done((f32[16,1536]{1,0:T(8,128)S(1)}, f32[16,1536]{1,0:T(8,128)S(1)}, u32[]{:S(2)}, u32[]{:S(2)}) %collective-permute-start.30) | collective-permute-done | bytes 98336 | tf_op jit(solution)/shard_map/ppermute | solution.py:44
  103.1 1.3 %collective-permute-done.25 = f32[32,2560]{1,0:T(8,128)S(1)} collective-permute-done((f32[32,2560]{1,0:T(8,128)S(1)}, f32[32,2560]{1,0:T(8,128)S(1)}, u32[]{:S(2)}, u32[]{:S(2)}) %collective-permute-start.25) | collective-permute-done | bytes 327712 | tf_op jit(solution)/shard_map/ppermute | solution.py:44
  104.4 0.1 add_add_fusion.1
  104.5 0.8 maximum_divide_fusion
  (30 shorter events, 0.4 us)
Async XLA Ops:
  1.0 10.1 %collective-permute-start.2 = (f32[80,1024]{1,0:T(8,128)S(1)}, f32[80,1024]{1,0:T(8,128)S(1)}, u32[]{:S(2)}, u32[]{:S(2)}) collective-permute-start(f32[80,1024]{1,0:T(8,128)S(1)} %pad_maximum_fusion.refs_0_), channel_id=1, source_target_pairs={{0,6},{1,7},{2,0},{3,1},{4,2},{5,3},{6,4},{7,5},{8,14},{9,15},{10,... | collective-permute-start | bytes 983048 | tf_op jit(solution)/shard_map/ppermute | solution.py:35
  4.2 10.4 %collective-permute-start.1 = (f32[80,1024]{1,0:T(8,128)S(1)}, f32[80,1024]{1,0:T(8,128)S(1)}, u32[]{:S(2)}, u32[]{:S(2)}) collective-permute-start(f32[80,1024]{1,0:T(8,128)S(1)} %pad_maximum_fusion.refs_0_), channel_id=1, source_target_pairs={{0,2},{1,3},{2,4},{3,5},{4,6},{5,7},{6,0},{7,1},{8,10},{9,11},{10,... | collective-permute-start | bytes 983048 | tf_op jit(solution)/shard_map/ppermute | solution.py:35
  4.2 10.7 %collective-permute-start = (f32[80,1024]{1,0:T(8,128)S(1)}, f32[80,1024]{1,0:T(8,128)S(1)}, u32[]{:S(2)}, u32[]{:S(2)}) collective-permute-start(f32[80,1024]{1,0:T(8,128)S(1)} %pad_maximum_fusion.refs_0_), channel_id=1, source_target_pairs={{0,8},{1,9},{2,10},{3,11},{4,12},{5,13},{6,14},{7,15},{8,0},{9,1},... | collective-permute-start | bytes 983048 | tf_op jit(solution)/shard_map/ppermute | solution.py:35
  7.2 11.3 %collective-permute-start.3 = (f32[80,1024]{1,0:T(8,128)S(1)}, f32[80,1024]{1,0:T(8,128)S(1)}, u32[]{:S(2)}, u32[]{:S(2)}) collective-permute-start(f32[80,1024]{1,0:T(8,128)S(1)} %pad_maximum_fusion.refs_0_), channel_id=1, source_target_pairs={{0,1},{1,0},{2,3},{3,2},{4,5},{5,4},{6,7},{7,6},{8,9},{9,8},{10,11... | collective-permute-start | bytes 983048 | tf_op jit(solution)/shard_map/ppermute | solution.py:35
  14.9 3.8 %collective-permute-start.4 = (f32[80,1024]{1,0:T(8,128)S(1)}, f32[80,1024]{1,0:T(8,128)S(1)}, u32[]{:S(2)}, u32[]{:S(2)}) collective-permute-start(f32[80,1024]{1,0:T(8,128)S(1)} %collective-permute-done.refs_1_), channel_id=1, source_target_pairs={{0,1},{1,0},{2,3},{3,2},{4,5},{5,4},{6,7},{7,6},{8,9},{9,8},{10,11... | collective-permute-start | bytes 983048 | tf_op jit(solution)/shard_map/ppermute | solution.py:35
  15.0 21.8 %collective-permute-start.9 = (f32[80,1024]{1,0:T(8,128)S(1)}, f32[80,1024]{1,0:T(8,128)S(1)}, u32[]{:S(2)}, u32[]{:S(2)}) collective-permute-start(f32[80,1024]{1,0:T(8,128)S(1)} %collective-permute-done.1.refs_0_.refs_6_), channel_id=1, source_target_pairs={{0,1},{1,0},{2,3},{3,2},{4,5},{5,4},{6,7},{7,6},{8,9},{9,8},{10,11... | collective-permute-start | bytes 983048 | tf_op jit(solution)/shard_map/ppermute | solution.py:35
  15.5 18.4 %collective-permute-start.6 = (f32[80,1024]{1,0:T(8,128)S(1)}, f32[80,1024]{1,0:T(8,128)S(1)}, u32[]{:S(2)}, u32[]{:S(2)}) collective-permute-start(f32[80,1024]{1,0:T(8,128)S(1)} %collective-permute-done.refs_1_), channel_id=1, source_target_pairs={{0,6},{1,7},{2,0},{3,1},{4,2},{5,3},{6,4},{7,5},{8,14},{9,15},{10,... | collective-permute-start | bytes 983048 | tf_op jit(solution)/shard_map/ppermute | solution.py:35
  18.5 15.4 %collective-permute-start.5 = (f32[80,1024]{1,0:T(8,128)S(1)}, f32[80,1024]{1,0:T(8,128)S(1)}, u32[]{:S(2)}, u32[]{:S(2)}) collective-permute-start(f32[80,1024]{1,0:T(8,128)S(1)} %collective-permute-done.refs_1_), channel_id=1, source_target_pairs={{0,2},{1,3},{2,4},{3,5},{4,6},{5,7},{6,0},{7,1},{8,10},{9,11},{10,... | collective-permute-start | bytes 983048 | tf_op jit(solution)/shard_map/ppermute | solution.py:35
  18.5 15.4 %collective-permute-start.7 = (f32[32,1024]{1,0:T(8,128)S(1)}, f32[32,1024]{1,0:T(8,128)S(1)}, u32[]{:S(2)}, u32[]{:S(2)}) collective-permute-start(f32[32,1024]{1,0:T(8,128)S(1)} %slice.60), channel_id=1, source_target_pairs={{0,2},{1,3},{2,4},{3,5},{4,6},{5,7},{6,0},{7,1},{8,10},{9,11},{10,... | collective-permute-start | bytes 393224 | tf_op jit(solution)/shard_map/ppermute | solution.py:35
  18.6 15.3 %collective-permute-start.8 = (f32[48,1024]{1,0:T(8,128)S(1)}, f32[48,1024]{1,0:T(8,128)S(1)}, u32[]{:S(2)}, u32[]{:S(2)}) collective-permute-start(f32[48,1024]{1,0:T(8,128)S(1)} %slice.61), channel_id=1, source_target_pairs={{0,6},{1,7},{2,0},{3,1},{4,2},{5,3},{6,4},{7,5},{8,14},{9,15},{10,... | collective-permute-start | bytes 589832 | tf_op jit(solution)/shard_map/ppermute | solution.py:35
  21.9 5.8 %copy-start = (f32[1,4096,1024]{2,1,0:T(8,128)S(1)}, f32[1,4096,1024]{2,1,0:T(8,128)}, u32[]{:S(2)}) copy-start(f32[1,4096,1024]{2,1,0:T(8,128)} %param.5) | copy-start | bytes 50331652
  27.7 9.3 %copy-start.1 = (f32[1,4096,1024]{2,1,0:T(8,128)S(1)}, f32[1,4096,1024]{2,1,0:T(8,128)}, u32[]{:S(2)}) copy-start(f32[1,4096,1024]{2,1,0:T(8,128)} %param.5) | copy-start | bytes 50331652
  33.9 2.8 %collective-permute-start.10 = (f32[80,1024]{1,0:T(8,128)S(1)}, f32[80,1024]{1,0:T(8,128)S(1)}, u32[]{:S(2)}, u32[]{:S(2)}) collective-permute-start(f32[80,1024]{1,0:T(8,128)S(1)} %collective-permute-done.5.refs_1_.refs_7_), channel_id=1, source_target_pairs={{0,1},{1,0},{2,3},{3,2},{4,5},{5,4},{6,7},{7,6},{8,9},{9,8},{10,11... | collective-permute-start | bytes 983048 | tf_op jit(solution)/shard_map/ppermute | solution.py:35
  34.0 11.4 %collective-permute-start.11 = (f32[80,1024]{1,0:T(8,128)S(1)}, f32[80,1024]{1,0:T(8,128)S(1)}, u32[]{:S(2)}, u32[]{:S(2)}) collective-permute-start(f32[80,1024]{1,0:T(8,128)S(1)} %collective-permute-done.2.refs_12_), channel_id=1, source_target_pairs={{0,1},{1,0},{2,3},{3,2},{4,5},{5,4},{6,7},{7,6},{8,9},{9,8},{10,11... | collective-permute-start | bytes 983048 | tf_op jit(solution)/shard_map/ppermute | solution.py:35
  34.6 12.0 %collective-permute-start.12 = (f32[80,1024]{1,0:T(8,128)S(1)}, f32[80,1024]{1,0:T(8,128)S(1)}, u32[]{:S(2)}, u32[]{:S(2)}) collective-permute-start(f32[80,1024]{1,0:T(8,128)S(1)} %collective-permute-done.6.refs_13_), channel_id=1, source_target_pairs={{0,1},{1,0},{2,3},{3,2},{4,5},{5,4},{6,7},{7,6},{8,9},{9,8},{10,11... | collective-permute-start | bytes 983048 | tf_op jit(solution)/shard_map/ppermute | solution.py:35
  34.7 8.6 %collective-permute-start.13 = (f32[32,1024]{1,0:T(8,128)S(1)}, f32[32,1024]{1,0:T(8,128)S(1)}, u32[]{:S(2)}, u32[]{:S(2)}) collective-permute-start(f32[32,1024]{1,0:T(8,128)S(1)} %slice.62), channel_id=1, source_target_pairs={{0,6},{1,7},{2,0},{3,1},{4,2},{5,3},{6,4},{7,5},{8,14},{9,15},{10,... | collective-permute-start | bytes 393224 | tf_op jit(solution)/shard_map/ppermute | solution.py:35
  36.8 8.2 %collective-permute-start.14 = (f32[48,1024]{1,0:T(8,128)S(1)}, f32[48,1024]{1,0:T(8,128)S(1)}, u32[]{:S(2)}, u32[]{:S(2)}) collective-permute-start(f32[48,1024]{1,0:T(8,128)S(1)} %slice.63), channel_id=1, source_target_pairs={{0,2},{1,3},{2,4},{3,5},{4,6},{5,7},{6,0},{7,1},{8,10},{9,11},{10,... | collective-permute-start | bytes 589832 | tf_op jit(solution)/shard_map/ppermute | solution.py:35
  36.8 9.8 %collective-permute-start.16 = (f32[48,1024]{1,0:T(8,128)S(1)}, f32[48,1024]{1,0:T(8,128)S(1)}, u32[]{:S(2)}, u32[]{:S(2)}) collective-permute-start(f32[48,1024]{1,0:T(8,128)S(1)} %collective-permute-done.8.refs_17_), channel_id=1, source_target_pairs={{0,1},{1,0},{2,3},{3,2},{4,5},{5,4},{6,7},{7,6},{8,9},{9,8},{10,11... | collective-permute-start | bytes 589832 | tf_op jit(solution)/shard_map/ppermute | solution.py:35
  44.9 1.9 %collective-permute-start.18 = (f32[48,1024]{1,0:T(8,128)S(1)}, f32[48,1024]{1,0:T(8,128)S(1)}, u32[]{:S(2)}, u32[]{:S(2)}) collective-permute-start(f32[48,1024]{1,0:T(8,128)S(1)} %collective-permute-done.14.refs_19_), channel_id=1, source_target_pairs={{0,1},{1,0},{2,3},{3,2},{4,5},{5,4},{6,7},{7,6},{8,9},{9,8},{10,11... | collective-permute-start | bytes 589832 | tf_op jit(solution)/shard_map/ppermute | solution.py:35
  44.9 1.6 %collective-permute-start.15 = (f32[32,1024]{1,0:T(8,128)S(1)}, f32[32,1024]{1,0:T(8,128)S(1)}, u32[]{:S(2)}, u32[]{:S(2)}) collective-permute-start(f32[32,1024]{1,0:T(8,128)S(1)} %collective-permute-done.7.refs_16_), channel_id=1, source_target_pairs={{0,1},{1,0},{2,3},{3,2},{4,5},{5,4},{6,7},{7,6},{8,9},{9,8},{10,11... | collective-permute-start | bytes 393224 | tf_op jit(solution)/shard_map/ppermute | solution.py:35
  45.5 1.3 %collective-permute-start.17 = (f32[32,1024]{1,0:T(8,128)S(1)}, f32[32,1024]{1,0:T(8,128)S(1)}, u32[]{:S(2)}, u32[]{:S(2)}) collective-permute-start(f32[32,1024]{1,0:T(8,128)S(1)} %collective-permute-done.13.refs_18_), channel_id=1, source_target_pairs={{0,1},{1,0},{2,3},{3,2},{4,5},{5,4},{6,7},{7,6},{8,9},{9,8},{10,11... | collective-permute-start | bytes 393224 | tf_op jit(solution)/shard_map/ppermute | solution.py:35
  58.1 19.2 %collective-permute-start.19 = (f32[64,2560]{1,0:T(8,128)S(1)}, f32[64,2560]{1,0:T(8,128)S(1)}, u32[]{:S(2)}, u32[]{:S(2)}) collective-permute-start(f32[64,2560]{1,0:T(8,128)S(1)} %get-tuple-element.78), channel_id=1, source_target_pairs={{0,16},{16,32},{32,48},{48,0},{64,80},{80,96},{96,112},{112,64},{1... | collective-permute-start | bytes 1966088 | tf_op jit(solution)/shard_map/ppermute | solution.py:44
  60.1 17.2 %collective-permute-start.20 = (f32[64,2560]{1,0:T(8,128)S(1)}, f32[64,2560]{1,0:T(8,128)S(1)}, u32[]{:S(2)}, u32[]{:S(2)}) collective-permute-start(f32[64,2560]{1,0:T(8,128)S(1)} %get-tuple-element.79), channel_id=1, source_target_pairs={{0,48},{16,0},{32,16},{48,32},{64,112},{80,64},{96,80},{112,96},{1... | collective-permute-start | bytes 1966088 | tf_op jit(solution)/shard_map/ppermute | solution.py:44
  62.3 19.4 %collective-permute-start.26 = (f32[128,1536]{1,0:T(8,128)S(1)}, f32[128,1536]{1,0:T(8,128)S(1)}, u32[]{:S(2)}, u32[]{:S(2)}) collective-permute-start(f32[128,1536]{1,0:T(8,128)S(1)} %get-tuple-element.87), channel_id=1, source_target_pairs={{0,64},{16,80},{32,96},{48,112},{64,0},{80,16},{96,32},{112,48},{1... | collective-permute-start | bytes 2359304 | tf_op jit(solution)/shard_map/ppermute | solution.py:44
  77.3 14.4 %collective-permute-start.23 = (f32[32,2560]{1,0:T(8,128)S(1)}, f32[32,2560]{1,0:T(8,128)S(1)}, u32[]{:S(2)}, u32[]{:S(2)}) collective-permute-start(f32[32,2560]{1,0:T(8,128)S(1)} %slice_add_fusion.1), channel_id=1, source_target_pairs={{0,16},{16,32},{32,48},{48,0},{64,80},{80,96},{96,112},{112,64},{1... | collective-permute-start | bytes 983048 | tf_op jit(solution)/shard_map/ppermute | solution.py:44
  78.7 13.0 %collective-permute-start.24 = (f32[32,2560]{1,0:T(8,128)S(1)}, f32[32,2560]{1,0:T(8,128)S(1)}, u32[]{:S(2)}, u32[]{:S(2)}) collective-permute-start(f32[32,2560]{1,0:T(8,128)S(1)} %slice_add_fusion), channel_id=1, source_target_pairs={{0,48},{16,0},{32,16},{48,32},{64,112},{80,64},{96,80},{112,96},{1... | collective-permute-start | bytes 983048 | tf_op jit(solution)/shard_map/ppermute | solution.py:44
  81.8 10.0 %collective-permute-start.28 = (f32[32,1536]{1,0:T(8,128)S(1)}, f32[32,1536]{1,0:T(8,128)S(1)}, u32[]{:S(2)}, u32[]{:S(2)}) collective-permute-start(f32[32,1536]{1,0:T(8,128)S(1)} %get-tuple-element.93), channel_id=1, source_target_pairs={{0,48},{16,0},{32,16},{48,32},{64,112},{80,64},{96,80},{112,96},{1... | collective-permute-start | bytes 589832 | tf_op jit(solution)/shard_map/ppermute | solution.py:44
  83.5 8.6 %collective-permute-start.27 = (f32[32,1536]{1,0:T(8,128)S(1)}, f32[32,1536]{1,0:T(8,128)S(1)}, u32[]{:S(2)}, u32[]{:S(2)}) collective-permute-start(f32[32,1536]{1,0:T(8,128)S(1)} %get-tuple-element.94), channel_id=1, source_target_pairs={{0,16},{16,32},{32,48},{48,0},{64,80},{80,96},{96,112},{112,64},{1... | collective-permute-start | bytes 589832 | tf_op jit(solution)/shard_map/ppermute | solution.py:44
  83.9 3.7 %collective-permute-start.21 = (f32[1,4096]{1,0:T(1,128)S(1)}, f32[1,4096]{1,0:T(1,128)S(1)}, u32[]{:S(2)}, u32[]{:S(2)}) collective-permute-start(f32[1,4096]{1,0:T(1,128)S(1)} %add_add_fusion.2), channel_id=1, source_target_pairs={{0,64},{16,80},{32,96},{48,112},{64,0},{80,16},{96,32},{112,48},{1... | collective-permute-start | bytes 49160 | tf_op jit(solution)/shard_map/ppermute | solution.py:44
  87.6 4.1 %collective-permute-start.22 = (f32[1,4096]{1,0:T(1,128)S(1)}, f32[1,4096]{1,0:T(1,128)S(1)}, u32[]{:S(2)}, u32[]{:S(2)}) collective-permute-start(f32[1,4096]{1,0:T(1,128)S(1)} %add.66), channel_id=1, source_target_pairs={{0,16},{16,0},{32,48},{48,32},{64,80},{80,64},{96,112},{112,96},{1... | collective-permute-start | bytes 49160 | tf_op jit(solution)/shard_map/ppermute | solution.py:44
  92.1 6.2 %collective-permute-start.29 = (f32[16,1536]{1,0:T(8,128)S(1)}, f32[16,1536]{1,0:T(8,128)S(1)}, u32[]{:S(2)}, u32[]{:S(2)}) collective-permute-start(f32[16,1536]{1,0:T(8,128)S(1)} %slice_add_fusion.4), channel_id=1, source_target_pairs={{0,16},{16,32},{32,48},{48,0},{64,80},{80,96},{96,112},{112,64},{1... | collective-permute-start | bytes 294920 | tf_op jit(solution)/shard_map/ppermute | solution.py:44
  93.3 6.7 %collective-permute-start.31 = (f32[1,4096]{1,0:T(1,128)S(1)}, f32[1,4096]{1,0:T(1,128)S(1)}, u32[]{:S(2)}, u32[]{:S(2)}) collective-permute-start(f32[1,4096]{1,0:T(1,128)S(1)} %add.67), channel_id=1, source_target_pairs={{0,32},{16,48},{32,0},{48,16},{64,96},{80,112},{96,64},{112,80},{1... | collective-permute-start | bytes 49160 | tf_op jit(solution)/shard_map/ppermute | solution.py:44
  96.9 7.5 %collective-permute-start.25 = (f32[32,2560]{1,0:T(8,128)S(1)}, f32[32,2560]{1,0:T(8,128)S(1)}, u32[]{:S(2)}, u32[]{:S(2)}) collective-permute-start(f32[32,2560]{1,0:T(8,128)S(1)} %add_add_fusion), channel_id=1, source_target_pairs={{0,64},{16,80},{32,96},{48,112},{64,0},{80,16},{96,32},{112,48},{1... | collective-permute-start | bytes 983048 | tf_op jit(solution)/shard_map/ppermute | solution.py:44
  98.4 4.7 %collective-permute-start.30 = (f32[16,1536]{1,0:T(8,128)S(1)}, f32[16,1536]{1,0:T(8,128)S(1)}, u32[]{:S(2)}, u32[]{:S(2)}) collective-permute-start(f32[16,1536]{1,0:T(8,128)S(1)} %get-tuple-element.92), channel_id=1, source_target_pairs={{0,48},{16,0},{32,16},{48,32},{64,112},{80,64},{96,80},{112,96},{1... | collective-permute-start | bytes 294920 | tf_op jit(solution)/shard_map/ppermute | solution.py:44

commit v3 on v2

--- a/solution.py
+++ b/solution.py
@@ -12,8 +12,7 @@
 ROWS = 64
 QROWS = 16
 PIECE = ROWS + QROWS
-TILE = 1024
-RAW_TILE = 512
+TILE = 2048
 SPLIT = (2560, 1536)
 BF16 = jnp.bfloat16
 F32 = jnp.float32
@@ -212,10 +211,12 @@
 
 
 def raw_kernel(first, runs, rh_ref, rl_ref, s_ref, *outs):
-    @pl.loop(0, outs[0].shape[1] // RAW_TILE)
+    size = outs[0].shape[1] // 2
+
+    @pl.loop(0, 2)
     def _(i):
-        rows = pl.ds(pl.multiple_of(first + i * RAW_TILE, RAW_TILE), RAW_TILE)
-        cols = pl.ds(pl.multiple_of(i * RAW_TILE, RAW_TILE), RAW_TILE)
+        rows = pl.ds(pl.multiple_of(first + i * size, size), size)
+        cols = pl.ds(pl.multiple_of(i * size, size), size)
         s = s_ref[rows, :]
         sh = s.astype(BF16)
         sl = (s - sh.astype(F32)).astype(BF16)
@@ -274,7 +275,7 @@
     last_below, last_above = z_up(up2 + from_below[:32]), z_down(down2 + from_above[:32])
     sizes_sq = sizes_sq + swap_x(sizes_sq)
     home = home + came
-    sizes_sq = sizes_sq + layer_permute(sizes_sq, lambda x_lo, z: (x_lo, z ^ 1))
+    sizes_sq = sizes_sq + layer_permute(sizes_sq, lambda x_lo, z: (x_lo, z ^ 2))
     sizes_sq, last_below, last_above = tie(sizes_sq, last_below, last_above)
     here = mine[:32] + from_above[32:] + last_below
     there = mine[32:] + from_below[32:] + last_above
@@ -287,7 +288,7 @@
         [home[96:112] + from_above[16:] + last_below, home[112:] + from_below[16:] + last_above], axis=0
     )
 
-    root = jnp.sqrt(sizes_sq + layer_permute(sizes_sq, lambda x_lo, z: (x_lo, z ^ 2)))
+    root = jnp.sqrt(sizes_sq + layer_permute(sizes_sq, lambda x_lo, z: (x_lo, z ^ 1)))
     return jnp.concatenate([first, last], axis=1) / root
 
 

time: 106 us -> 104 us (0.981)
  starting transfers between devices: 37.1 us -> 35.6 us
    ppermute x13, starting transfers between devices: 20.5 us -> 19.1 us  [layer_permute(): return lax.ppermute(x, 'layer', pairs)]
  transfers between devices with their start and end apart: 32 -> 32, of which waited for: 13 -> 12; matrix products, arithmetic and copies ran while one was open for 1% -> 1% of each run, Pallas kernels for 22% -> 22%
where the time goes in v3:
time: 104 us
  starting transfers between devices  35.6 us (34%)
  Pallas kernels  33.6 us (32%)
  waiting for transfers between devices  26.3 us (25%)
  local copies, waits for them, and re-layouts  5.85 us (6%)
  other arithmetic  2.42 us (2%)
    ppermute x13, starting transfers between devices, layer_permute(): return lax.ppermute(x, 'layer', pairs)  19.1 us
    ppermute x19, starting transfers between devices, example_permute(): return lax.ppermute(x, 'example', pairs)  16.5 us
    ppermute x13, waiting for transfers between devices, layer_permute(): return lax.ppermute(x, 'layer', pairs)  15.5 us
    pallas_call x2, Pallas kernels, part_sizes(): pl.pallas_call(functools.partial(part_kernel, blocks, y_shift, len(buffer...  12.3 us
    pallas_call x1, Pallas kernels, rest_sizes(): pl.pallas_call(functools.partial(rest_kernel, y_shifts), in_specs=[SMEM]...  10.9 us
    ppermute x19, waiting for transfers between devices, example_permute(): return lax.ppermute(x, 'example', pairs)  10.8 us
    pallas_call x2, Pallas kernels, raw_scores(): pl.pallas_call(functools.partial(raw_kernel, first, runs), in_specs=[VMEM...  7.36 us
    unnamed x4, local copies, waits for them, and re-layouts  5.77 us
  transfers between devices with their start and end apart: 32, of which 12 were waited for; matrix products, arithmetic and copies ran while one was open for 1% of the time, Pallas kernels for 22%

profile of v3, /device:TPU:0, one launch (start us, length us, event | category | flops | bytes accessed | tf_op | source)
XLA Modules:
  0.0 104.1 jit_solution(5233904045345445310)
XLA Ops:
  0.0 1.0 pad_maximum_fusion.refs_0_
  1.0 3.2 %collective-permute-start.2 = (f32[80,1024]{1,0:T(8,128)S(1)}, f32[80,1024]{1,0:T(8,128)S(1)}, u32[]{:S(2)}, u32[]{:S(2)}) collective-permute-start(f32[80,1024]{1,0:T(8,128)S(1)} %pad_maximum_fusion.refs_0_), channel_id=1, source_target_pairs={{0,6},{1,7},{2,0},{3,1},{4,2},{5,3},{6,4},{7,5},{8,14},{9,15},{10,... | collective-permute-start | bytes 983048 | tf_op jit(solution)/shard_map/ppermute | solution.py:34
  4.2 3.0 %collective-permute-start = (f32[80,1024]{1,0:T(8,128)S(1)}, f32[80,1024]{1,0:T(8,128)S(1)}, u32[]{:S(2)}, u32[]{:S(2)}) collective-permute-start(f32[80,1024]{1,0:T(8,128)S(1)} %pad_maximum_fusion.refs_0_), channel_id=1, source_target_pairs={{0,8},{1,9},{2,10},{3,11},{4,12},{5,13},{6,14},{7,15},{8,0},{9,1},... | collective-permute-start | bytes 983048 | tf_op jit(solution)/shard_map/ppermute | solution.py:34
  7.2 0.0 collective-permute-start.3
  7.2 3.9 %collective-permute-done.2.refs_12_ = f32[80,1024]{1,0:T(8,128)S(1)} collective-permute-done((f32[80,1024]{1,0:T(8,128)S(1)}, f32[80,1024]{1,0:T(8,128)S(1)}, u32[]{:S(2)}, u32[]{:S(2)}) %collective-permute-start.2) | collective-permute-done | bytes 327712 | tf_op jit(solution)/shard_map/ppermute | solution.py:34
  11.2 3.4 %collective-permute-done.1.refs_0_.refs_6_ = f32[80,1024]{1,0:T(8,128)S(1)} collective-permute-done((f32[80,1024]{1,0:T(8,128)S(1)}, f32[80,1024]{1,0:T(8,128)S(1)}, u32[]{:S(2)}, u32[]{:S(2)}) %collective-permute-start.1) | collective-permute-done | bytes 327712 | tf_op jit(solution)/shard_map/ppermute | solution.py:34
  14.6 0.3 collective-permute-done.refs_1_
  14.9 0.1 pad_add_fusion.where_ref
  15.0 0.6 collective-permute-start.9
  15.5 3.0 %collective-permute-start.6 = (f32[80,1024]{1,0:T(8,128)S(1)}, f32[80,1024]{1,0:T(8,128)S(1)}, u32[]{:S(2)}, u32[]{:S(2)}) collective-permute-start(f32[80,1024]{1,0:T(8,128)S(1)} %collective-permute-done.refs_1_), channel_id=1, source_target_pairs={{0,6},{1,7},{2,0},{3,1},{4,2},{5,3},{6,4},{7,5},{8,14},{9,15},{10,... | collective-permute-start | bytes 983048 | tf_op jit(solution)/shard_map/ppermute | solution.py:34
  18.5 0.0 collective-permute-done.3.refs_2_
  18.5 0.1 collective-permute-start.7
  18.6 3.3 %collective-permute-start.8 = (f32[48,1024]{1,0:T(8,128)S(1)}, f32[48,1024]{1,0:T(8,128)S(1)}, u32[]{:S(2)}, u32[]{:S(2)}) collective-permute-start(f32[48,1024]{1,0:T(8,128)S(1)} %slice.61), channel_id=1, source_target_pairs={{0,6},{1,7},{2,0},{3,1},{4,2},{5,3},{6,4},{7,5},{8,14},{9,15},{10,... | collective-permute-start | bytes 589832 | tf_op jit(solution)/shard_map/ppermute | solution.py:34
  21.9 5.8 %copy-done = f32[1,4096,1024]{2,1,0:T(8,128)S(1)} copy-done((f32[1,4096,1024]{2,1,0:T(8,128)S(1)}, f32[1,4096,1024]{2,1,0:T(8,128)}, u32[]{:S(2)}) %copy-start) | copy-done | bytes 16777240
  27.7 6.2 %shard_map.37 = (bf16[256,1024]{1,0:T(8,128)(2,1)S(1)}, bf16[256,1024]{1,0:T(8,128)(2,1)S(1)}, f32[1,4096]{1,0:T(1,128)S(1)}) custom-call(s32[3]{0:T(128)S(1)} %pad_add_fusion.where_ref, f32[80,1024]{1,0:T(8,128)S(1)} %pad_maximum_fusion.refs_0_, f32[80,1024]{1,0:T(8,128)S(1)} %collective-permute-done.refs_1_, ...), custom_call_target="tpu_custom_call" | custom-call | flops 8589934592 | bytes 16777216 | tf_op jit(solution)/shard_map/pallas_call | solution.py:121
  33.9 0.0 collective-permute-done.7.refs_16_
  33.9 0.0 collective-permute-done.8.refs_17_
  34.0 0.1 collective-permute-start.10
  34.0 0.5 collective-permute-start.11
  34.6 0.2 collective-permute-start.12
  34.7 1.8 %collective-permute-start.13 = (f32[32,1024]{1,0:T(8,128)S(1)}, f32[32,1024]{1,0:T(8,128)S(1)}, u32[]{:S(2)}, u32[]{:S(2)}) collective-permute-start(f32[32,1024]{1,0:T(8,128)S(1)} %slice.62), channel_id=1, source_target_pairs={{0,6},{1,7},{2,0},{3,1},{4,2},{5,3},{6,4},{7,5},{8,14},{9,15},{10,... | collective-permute-start | bytes 393224 | tf_op jit(solution)/shard_map/ppermute | solution.py:34
  36.6 0.0 collective-permute-done.9.refs_2_.refs_8_
  36.6 0.2 collective-permute-start.14
  36.8 0.0 collective-permute-start.16
  36.8 6.1 %shard_map.38 = (bf16[256,1024]{1,0:T(8,128)(2,1)S(1)}, bf16[256,1024]{1,0:T(8,128)(2,1)S(1)}, f32[1,4096]{1,0:T(1,128)S(1)}) custom-call(s32[3]{0:T(128)S(1)} %pad_add_fusion.where_ref, f32[80,1024]{1,0:T(8,128)S(1)} %collective-permute-done.1.refs_0_.refs_6_, f32[80,1024]{1,0:T(8,128)S(1)} %collective-permute-done.5.refs_1_.refs_7_, ...), custom_call_target="tpu_custom_call" | custom-call | flops 8589934592 | bytes 16777216 | tf_op jit(solution)/shard_map/pallas_call | solution.py:121
  43.0 0.0 collective-permute-done.13.refs_18_
  43.0 1.8 %collective-permute-done.14.refs_19_ = f32[48,1024]{1,0:T(8,128)S(1)} collective-permute-done((f32[48,1024]{1,0:T(8,128)S(1)}, f32[48,1024]{1,0:T(8,128)S(1)}, u32[]{:S(2)}, u32[]{:S(2)}) %collective-permute-start.14) | collective-permute-done | bytes 196640 | tf_op jit(solution)/shard_map/ppermute | solution.py:34
  44.8 0.0 collective-permute-start.18
  44.8 0.5 collective-permute-start.15
  45.3 0.0 collective-permute-done.11.refs_14_
  45.3 0.0 collective-permute-start.17
  45.3 1.1 %collective-permute-done.15.refs_20_ = f32[32,1024]{1,0:T(8,128)S(1)} collective-permute-done((f32[32,1024]{1,0:T(8,128)S(1)}, f32[32,1024]{1,0:T(8,128)S(1)}, u32[]{:S(2)}, u32[]{:S(2)}) %collective-permute-start.15) | collective-permute-done | bytes 131104 | tf_op jit(solution)/shard_map/ppermute | solution.py:34
  46.4 0.0 collective-permute-done.16.refs_21_
  46.4 0.0 collective-permute-done.12.refs_15_
  46.4 0.2 collective-permute-done.17.refs_22_
  46.6 3.0 %shard_map.39 = (bf16[256,1024]{1,0:T(8,128)(2,1)S(1)}, bf16[256,1024]{1,0:T(8,128)(2,1)S(1)}, bf16[256,1024]{1,0:T(8,128)(2,1)S(1)}, bf16[256,1024]{1,0:T(8,128...) custom-call(s32[3]{0:T(128)S(1)} %pad_add_fusion.where_ref, ...), custom_call_target="tpu_custom_call" | custom-call | flops 1610612736 | bytes 1048576 | tf_op jit(solution)/shard_map/pallas_call | solution.py:197
  49.7 4.5 %shard_map.40 = (f32[64,2560]{1,0:T(8,128)S(1)}, f32[64,2560]{1,0:T(8,128)S(1)}, f32[32,2560]{1,0:T(8,128)S(1)}, f32[32,2560]{1,0:T(8,128)S(1)}, f32[64,2560]{1,0:T(8,128)S(1)}) custom-call(bf16[256,1024]{1,0:T(8,128)(2,1)S(1)} %get-tuple-element.72.rh_ref, bf16[256,1024]{1,0:T(8,128)(2,1)S(1)} %get-tuple-element.64.rl_ref, f32[4096,1024]{1,0:T(8,128)S(1)} %bitcast.9), custom_call_target="tpu_custom_call" | custom-call | flops 5368709120 | bytes 13107200 | tf_op jit(solution)/shard_map/pallas_call | solution.py:232
  54.2 2.9 %shard_map.41 = (f32[128,1536]{1,0:T(8,128)S(1)}, f32[128,1536]{1,0:T(8,128)S(1)}) custom-call(bf16[256,1024]{1,0:T(8,128)(2,1)S(1)} %get-tuple-element.72.rh_ref, bf16[256,1024]{1,0:T(8,128)(2,1)S(1)} %get-tuple-element.64.rl_ref, f32[4096,1024]{1,0:T(8,128)S(1)} %bitcast.10), custom_call_target="tpu_custom_call" | custom-call | flops 3221225472 | bytes 7864320 | tf_op jit(solution)/shard_map/pallas_call | solution.py:232
  57.0 2.0 %collective-permute-start.19 = (f32[64,2560]{1,0:T(8,128)S(1)}, f32[64,2560]{1,0:T(8,128)S(1)}, u32[]{:S(2)}, u32[]{:S(2)}) collective-permute-start(f32[64,2560]{1,0:T(8,128)S(1)} %get-tuple-element.78), channel_id=1, source_target_pairs={{0,16},{16,32},{32,48},{48,0},{64,80},{80,96},{96,112},{112,64},{1... | collective-permute-start | bytes 1966088 | tf_op jit(solution)/shard_map/ppermute | solution.py:43
  59.0 2.2 %collective-permute-start.20 = (f32[64,2560]{1,0:T(8,128)S(1)}, f32[64,2560]{1,0:T(8,128)S(1)}, u32[]{:S(2)}, u32[]{:S(2)}) collective-permute-start(f32[64,2560]{1,0:T(8,128)S(1)} %get-tuple-element.79), channel_id=1, source_target_pairs={{0,48},{16,0},{32,16},{48,32},{64,112},{80,64},{96,80},{112,96},{1... | collective-permute-start | bytes 1966088 | tf_op jit(solution)/shard_map/ppermute | solution.py:43
  61.2 1.5 %collective-permute-start.26 = (f32[128,1536]{1,0:T(8,128)S(1)}, f32[128,1536]{1,0:T(8,128)S(1)}, u32[]{:S(2)}, u32[]{:S(2)}) collective-permute-start(f32[128,1536]{1,0:T(8,128)S(1)} %get-tuple-element.87), channel_id=1, source_target_pairs={{0,64},{16,80},{32,96},{48,112},{64,0},{80,16},{96,32},{112,48},{1... | collective-permute-start | bytes 2359304 | tf_op jit(solution)/shard_map/ppermute | solution.py:43
  62.7 10.9 %shard_map.42 = f32[1,4096]{1,0:T(1,128)S(1)} custom-call(s32[3]{0:T(128)S(1)} %pad_add_fusion.where_ref, bf16[256,1024]{1,0:T(8,128)(2,1)S(1)} %get-tuple-element.74.refs_0_, bf16[256,1024]{1,0:T(8,128)(2,1)S(1)} %get-tuple-element.75.refs_1_, bf16[256,1024]{1,0:T(8,128)(2,1)S(1)} %get-tuple-element.76.refs_2_, ...), custom_call_target="tpu_custom_call" | custom-call | flops 1 | bytes 1 | tf_op jit(solution)/shard_map/pallas_call | solution.py:141
  73.7 2.6 %collective-permute-done.19 = f32[64,2560]{1,0:T(8,128)S(1)} collective-permute-done((f32[64,2560]{1,0:T(8,128)S(1)}, f32[64,2560]{1,0:T(8,128)S(1)}, u32[]{:S(2)}, u32[]{:S(2)}) %collective-permute-start.19) | collective-permute-done | bytes 655392 | tf_op jit(solution)/shard_map/ppermute | solution.py:43
  76.3 1.3 %collective-permute-start.23 = (f32[32,2560]{1,0:T(8,128)S(1)}, f32[32,2560]{1,0:T(8,128)S(1)}, u32[]{:S(2)}, u32[]{:S(2)}) collective-permute-start(f32[32,2560]{1,0:T(8,128)S(1)} %slice_add_fusion.1), channel_id=1, source_target_pairs={{0,16},{16,32},{32,48},{48,0},{64,80},{80,96},{96,112},{112,64},{1... | collective-permute-start | bytes 983048 | tf_op jit(solution)/shard_map/ppermute | solution.py:43
  77.6 2.1 %collective-permute-start.24 = (f32[32,2560]{1,0:T(8,128)S(1)}, f32[32,2560]{1,0:T(8,128)S(1)}, u32[]{:S(2)}, u32[]{:S(2)}) collective-permute-start(f32[32,2560]{1,0:T(8,128)S(1)} %slice_add_fusion), channel_id=1, source_target_pairs={{0,48},{16,0},{32,16},{48,32},{64,112},{80,64},{96,80},{112,96},{1... | collective-permute-start | bytes 983048 | tf_op jit(solution)/shard_map/ppermute | solution.py:43
  79.7 0.9 collective-permute-done.26
  80.6 0.1 add.74
  80.7 2.0 %collective-permute-start.28 = (f32[32,1536]{1,0:T(8,128)S(1)}, f32[32,1536]{1,0:T(8,128)S(1)}, u32[]{:S(2)}, u32[]{:S(2)}) collective-permute-start(f32[32,1536]{1,0:T(8,128)S(1)} %get-tuple-element.93), channel_id=1, source_target_pairs={{0,48},{16,0},{32,16},{48,32},{64,112},{80,64},{96,80},{112,96},{1... | collective-permute-start | bytes 589832 | tf_op jit(solution)/shard_map/ppermute | solution.py:43
  82.7 0.4 collective-permute-start.27
  83.0 1.5 %collective-permute-start.21 = (f32[1,4096]{1,0:T(1,128)S(1)}, f32[1,4096]{1,0:T(1,128)S(1)}, u32[]{:S(2)}, u32[]{:S(2)}) collective-permute-start(f32[1,4096]{1,0:T(1,128)S(1)} %add_add_fusion.2), channel_id=1, source_target_pairs={{0,64},{16,80},{32,96},{48,112},{64,0},{80,16},{96,32},{112,48},{1... | collective-permute-start | bytes 49160 | tf_op jit(solution)/shard_map/ppermute | solution.py:43
  84.5 2.2 %collective-permute-done.21 = f32[1,4096]{1,0:T(1,128)S(1)} collective-permute-done((f32[1,4096]{1,0:T(1,128)S(1)}, f32[1,4096]{1,0:T(1,128)S(1)}, u32[]{:S(2)}, u32[]{:S(2)}) %collective-permute-start.21) | collective-permute-done | bytes 16416 | tf_op jit(solution)/shard_map/ppermute | solution.py:43
  86.8 1.6 %collective-permute-start.22 = (f32[1,4096]{1,0:T(1,128)S(1)}, f32[1,4096]{1,0:T(1,128)S(1)}, u32[]{:S(2)}, u32[]{:S(2)}) collective-permute-start(f32[1,4096]{1,0:T(1,128)S(1)} %add.66), channel_id=1, source_target_pairs={{0,32},{16,48},{32,0},{48,16},{64,96},{80,112},{96,64},{112,80},{1... | collective-permute-start | bytes 49160 | tf_op jit(solution)/shard_map/ppermute | solution.py:43
  88.4 4.0 %collective-permute-done.22 = f32[1,4096]{1,0:T(1,128)S(1)} collective-permute-done((f32[1,4096]{1,0:T(1,128)S(1)}, f32[1,4096]{1,0:T(1,128)S(1)}, u32[]{:S(2)}, u32[]{:S(2)}) %collective-permute-start.22) | collective-permute-done | bytes 16416 | tf_op jit(solution)/shard_map/ppermute | solution.py:43
  92.4 0.0 collective-permute-done.23
  92.4 0.0 collective-permute-done.28
  92.5 1.3 %collective-permute-start.29 = (f32[16,1536]{1,0:T(8,128)S(1)}, f32[16,1536]{1,0:T(8,128)S(1)}, u32[]{:S(2)}, u32[]{:S(2)}) collective-permute-start(f32[16,1536]{1,0:T(8,128)S(1)} %slice_add_fusion.4), channel_id=1, source_target_pairs={{0,16},{16,32},{32,48},{48,0},{64,80},{80,96},{96,112},{112,64},{1... | collective-permute-start | bytes 294920 | tf_op jit(solution)/shard_map/ppermute | solution.py:43
  93.8 0.1 add_add_fusion
  93.9 0.4 collective-permute-start.31
  94.3 1.5 %collective-permute-start.25 = (f32[32,2560]{1,0:T(8,128)S(1)}, f32[32,2560]{1,0:T(8,128)S(1)}, u32[]{:S(2)}, u32[]{:S(2)}) collective-permute-start(f32[32,2560]{1,0:T(8,128)S(1)} %add_add_fusion), channel_id=1, source_target_pairs={{0,64},{16,80},{32,96},{48,112},{64,0},{80,16},{96,32},{112,48},{1... | collective-permute-start | bytes 983048 | tf_op jit(solution)/shard_map/ppermute | solution.py:43
  95.7 2.6 %collective-permute-done.29 = f32[16,1536]{1,0:T(8,128)S(1)} collective-permute-done((f32[16,1536]{1,0:T(8,128)S(1)}, f32[16,1536]{1,0:T(8,128)S(1)}, u32[]{:S(2)}, u32[]{:S(2)}) %collective-permute-start.29) | collective-permute-done | bytes 98336 | tf_op jit(solution)/shard_map/ppermute | solution.py:43
  98.4 1.5 %collective-permute-start.30 = (f32[16,1536]{1,0:T(8,128)S(1)}, f32[16,1536]{1,0:T(8,128)S(1)}, u32[]{:S(2)}, u32[]{:S(2)}) collective-permute-start(f32[16,1536]{1,0:T(8,128)S(1)} %get-tuple-element.92), channel_id=1, source_target_pairs={{0,48},{16,0},{32,16},{48,32},{64,112},{80,64},{96,80},{112,96},{1... | collective-permute-start | bytes 294920 | tf_op jit(solution)/shard_map/ppermute | solution.py:43
  99.9 3.2 %collective-permute-done.30 = f32[16,1536]{1,0:T(8,128)S(1)} collective-permute-done((f32[16,1536]{1,0:T(8,128)S(1)}, f32[16,1536]{1,0:T(8,128)S(1)}, u32[]{:S(2)}, u32[]{:S(2)}) %collective-permute-start.30) | collective-permute-done | bytes 98336 | tf_op jit(solution)/shard_map/ppermute | solution.py:43
  103.1 0.1 add_add_fusion.1
  103.2 0.8 maximum_divide_fusion
  (30 shorter events, 0.4 us)
Async XLA Ops:
  1.0 10.1 %collective-permute-start.2 = (f32[80,1024]{1,0:T(8,128)S(1)}, f32[80,1024]{1,0:T(8,128)S(1)}, u32[]{:S(2)}, u32[]{:S(2)}) collective-permute-start(f32[80,1024]{1,0:T(8,128)S(1)} %pad_maximum_fusion.refs_0_), channel_id=1, source_target_pairs={{0,6},{1,7},{2,0},{3,1},{4,2},{5,3},{6,4},{7,5},{8,14},{9,15},{10,... | collective-permute-start | bytes 983048 | tf_op jit(solution)/shard_map/ppermute | solution.py:34
  4.2 10.4 %collective-permute-start.1 = (f32[80,1024]{1,0:T(8,128)S(1)}, f32[80,1024]{1,0:T(8,128)S(1)}, u32[]{:S(2)}, u32[]{:S(2)}) collective-permute-start(f32[80,1024]{1,0:T(8,128)S(1)} %pad_maximum_fusion.refs_0_), channel_id=1, source_target_pairs={{0,2},{1,3},{2,4},{3,5},{4,6},{5,7},{6,0},{7,1},{8,10},{9,11},{10,... | collective-permute-start | bytes 983048 | tf_op jit(solution)/shard_map/ppermute | solution.py:34
  4.2 10.7 %collective-permute-start = (f32[80,1024]{1,0:T(8,128)S(1)}, f32[80,1024]{1,0:T(8,128)S(1)}, u32[]{:S(2)}, u32[]{:S(2)}) collective-permute-start(f32[80,1024]{1,0:T(8,128)S(1)} %pad_maximum_fusion.refs_0_), channel_id=1, source_target_pairs={{0,8},{1,9},{2,10},{3,11},{4,12},{5,13},{6,14},{7,15},{8,0},{9,1},... | collective-permute-start | bytes 983048 | tf_op jit(solution)/shard_map/ppermute | solution.py:34
  7.2 11.3 %collective-permute-start.3 = (f32[80,1024]{1,0:T(8,128)S(1)}, f32[80,1024]{1,0:T(8,128)S(1)}, u32[]{:S(2)}, u32[]{:S(2)}) collective-permute-start(f32[80,1024]{1,0:T(8,128)S(1)} %pad_maximum_fusion.refs_0_), channel_id=1, source_target_pairs={{0,1},{1,0},{2,3},{3,2},{4,5},{5,4},{6,7},{7,6},{8,9},{9,8},{10,11... | collective-permute-start | bytes 983048 | tf_op jit(solution)/shard_map/ppermute | solution.py:34
  14.9 3.8 %collective-permute-start.4 = (f32[80,1024]{1,0:T(8,128)S(1)}, f32[80,1024]{1,0:T(8,128)S(1)}, u32[]{:S(2)}, u32[]{:S(2)}) collective-permute-start(f32[80,1024]{1,0:T(8,128)S(1)} %collective-permute-done.refs_1_), channel_id=1, source_target_pairs={{0,1},{1,0},{2,3},{3,2},{4,5},{5,4},{6,7},{7,6},{8,9},{9,8},{10,11... | collective-permute-start | bytes 983048 | tf_op jit(solution)/shard_map/ppermute | solution.py:34
  15.0 21.6 %collective-permute-start.9 = (f32[80,1024]{1,0:T(8,128)S(1)}, f32[80,1024]{1,0:T(8,128)S(1)}, u32[]{:S(2)}, u32[]{:S(2)}) collective-permute-start(f32[80,1024]{1,0:T(8,128)S(1)} %collective-permute-done.1.refs_0_.refs_6_), channel_id=1, source_target_pairs={{0,1},{1,0},{2,3},{3,2},{4,5},{5,4},{6,7},{7,6},{8,9},{9,8},{10,11... | collective-permute-start | bytes 983048 | tf_op jit(solution)/shard_map/ppermute | solution.py:34
  15.5 18.4 %collective-permute-start.6 = (f32[80,1024]{1,0:T(8,128)S(1)}, f32[80,1024]{1,0:T(8,128)S(1)}, u32[]{:S(2)}, u32[]{:S(2)}) collective-permute-start(f32[80,1024]{1,0:T(8,128)S(1)} %collective-permute-done.refs_1_), channel_id=1, source_target_pairs={{0,6},{1,7},{2,0},{3,1},{4,2},{5,3},{6,4},{7,5},{8,14},{9,15},{10,... | collective-permute-start | bytes 983048 | tf_op jit(solution)/shard_map/ppermute | solution.py:34
  18.5 15.4 %collective-permute-start.5 = (f32[80,1024]{1,0:T(8,128)S(1)}, f32[80,1024]{1,0:T(8,128)S(1)}, u32[]{:S(2)}, u32[]{:S(2)}) collective-permute-start(f32[80,1024]{1,0:T(8,128)S(1)} %collective-permute-done.refs_1_), channel_id=1, source_target_pairs={{0,2},{1,3},{2,4},{3,5},{4,6},{5,7},{6,0},{7,1},{8,10},{9,11},{10,... | collective-permute-start | bytes 983048 | tf_op jit(solution)/shard_map/ppermute | solution.py:34
  18.5 15.4 %collective-permute-start.7 = (f32[32,1024]{1,0:T(8,128)S(1)}, f32[32,1024]{1,0:T(8,128)S(1)}, u32[]{:S(2)}, u32[]{:S(2)}) collective-permute-start(f32[32,1024]{1,0:T(8,128)S(1)} %slice.60), channel_id=1, source_target_pairs={{0,2},{1,3},{2,4},{3,5},{4,6},{5,7},{6,0},{7,1},{8,10},{9,11},{10,... | collective-permute-start | bytes 393224 | tf_op jit(solution)/shard_map/ppermute | solution.py:34
  18.6 15.3 %collective-permute-start.8 = (f32[48,1024]{1,0:T(8,128)S(1)}, f32[48,1024]{1,0:T(8,128)S(1)}, u32[]{:S(2)}, u32[]{:S(2)}) collective-permute-start(f32[48,1024]{1,0:T(8,128)S(1)} %slice.61), channel_id=1, source_target_pairs={{0,6},{1,7},{2,0},{3,1},{4,2},{5,3},{6,4},{7,5},{8,14},{9,15},{10,... | collective-permute-start | bytes 589832 | tf_op jit(solution)/shard_map/ppermute | solution.py:34
  21.9 5.8 %copy-start = (f32[1,4096,1024]{2,1,0:T(8,128)S(1)}, f32[1,4096,1024]{2,1,0:T(8,128)}, u32[]{:S(2)}) copy-start(f32[1,4096,1024]{2,1,0:T(8,128)} %param.5) | copy-start | bytes 50331652
  27.7 9.1 %copy-start.1 = (f32[1,4096,1024]{2,1,0:T(8,128)S(1)}, f32[1,4096,1024]{2,1,0:T(8,128)}, u32[]{:S(2)}) copy-start(f32[1,4096,1024]{2,1,0:T(8,128)} %param.5) | copy-start | bytes 50331652
  34.0 2.8 %collective-permute-start.10 = (f32[80,1024]{1,0:T(8,128)S(1)}, f32[80,1024]{1,0:T(8,128)S(1)}, u32[]{:S(2)}, u32[]{:S(2)}) collective-permute-start(f32[80,1024]{1,0:T(8,128)S(1)} %collective-permute-done.5.refs_1_.refs_7_), channel_id=1, source_target_pairs={{0,1},{1,0},{2,3},{3,2},{4,5},{5,4},{6,7},{7,6},{8,9},{9,8},{10,11... | collective-permute-start | bytes 983048 | tf_op jit(solution)/shard_map/ppermute | solution.py:34
  34.0 11.2 %collective-permute-start.11 = (f32[80,1024]{1,0:T(8,128)S(1)}, f32[80,1024]{1,0:T(8,128)S(1)}, u32[]{:S(2)}, u32[]{:S(2)}) collective-permute-start(f32[80,1024]{1,0:T(8,128)S(1)} %collective-permute-done.2.refs_12_), channel_id=1, source_target_pairs={{0,1},{1,0},{2,3},{3,2},{4,5},{5,4},{6,7},{7,6},{8,9},{9,8},{10,11... | collective-permute-start | bytes 983048 | tf_op jit(solution)/shard_map/ppermute | solution.py:34
  34.6 11.8 %collective-permute-start.12 = (f32[80,1024]{1,0:T(8,128)S(1)}, f32[80,1024]{1,0:T(8,128)S(1)}, u32[]{:S(2)}, u32[]{:S(2)}) collective-permute-start(f32[80,1024]{1,0:T(8,128)S(1)} %collective-permute-done.6.refs_13_), channel_id=1, source_target_pairs={{0,1},{1,0},{2,3},{3,2},{4,5},{5,4},{6,7},{7,6},{8,9},{9,8},{10,11... | collective-permute-start | bytes 983048 | tf_op jit(solution)/shard_map/ppermute | solution.py:34
  34.7 8.2 %collective-permute-start.13 = (f32[32,1024]{1,0:T(8,128)S(1)}, f32[32,1024]{1,0:T(8,128)S(1)}, u32[]{:S(2)}, u32[]{:S(2)}) collective-permute-start(f32[32,1024]{1,0:T(8,128)S(1)} %slice.62), channel_id=1, source_target_pairs={{0,6},{1,7},{2,0},{3,1},{4,2},{5,3},{6,4},{7,5},{8,14},{9,15},{10,... | collective-permute-start | bytes 393224 | tf_op jit(solution)/shard_map/ppermute | solution.py:34
  36.6 8.2 %collective-permute-start.14 = (f32[48,1024]{1,0:T(8,128)S(1)}, f32[48,1024]{1,0:T(8,128)S(1)}, u32[]{:S(2)}, u32[]{:S(2)}) collective-permute-start(f32[48,1024]{1,0:T(8,128)S(1)} %slice.63), channel_id=1, source_target_pairs={{0,2},{1,3},{2,4},{3,5},{4,6},{5,7},{6,0},{7,1},{8,10},{9,11},{10,... | collective-permute-start | bytes 589832 | tf_op jit(solution)/shard_map/ppermute | solution.py:34
  36.8 9.6 %collective-permute-start.16 = (f32[48,1024]{1,0:T(8,128)S(1)}, f32[48,1024]{1,0:T(8,128)S(1)}, u32[]{:S(2)}, u32[]{:S(2)}) collective-permute-start(f32[48,1024]{1,0:T(8,128)S(1)} %collective-permute-done.8.refs_17_), channel_id=1, source_target_pairs={{0,1},{1,0},{2,3},{3,2},{4,5},{5,4},{6,7},{7,6},{8,9},{9,8},{10,11... | collective-permute-start | bytes 589832 | tf_op jit(solution)/shard_map/ppermute | solution.py:34
  44.8 1.9 %collective-permute-start.18 = (f32[48,1024]{1,0:T(8,128)S(1)}, f32[48,1024]{1,0:T(8,128)S(1)}, u32[]{:S(2)}, u32[]{:S(2)}) collective-permute-start(f32[48,1024]{1,0:T(8,128)S(1)} %collective-permute-done.14.refs_19_), channel_id=1, source_target_pairs={{0,1},{1,0},{2,3},{3,2},{4,5},{5,4},{6,7},{7,6},{8,9},{9,8},{10,11... | collective-permute-start | bytes 589832 | tf_op jit(solution)/shard_map/ppermute | solution.py:34
  44.8 1.6 %collective-permute-start.15 = (f32[32,1024]{1,0:T(8,128)S(1)}, f32[32,1024]{1,0:T(8,128)S(1)}, u32[]{:S(2)}, u32[]{:S(2)}) collective-permute-start(f32[32,1024]{1,0:T(8,128)S(1)} %collective-permute-done.7.refs_16_), channel_id=1, source_target_pairs={{0,1},{1,0},{2,3},{3,2},{4,5},{5,4},{6,7},{7,6},{8,9},{9,8},{10,11... | collective-permute-start | bytes 393224 | tf_op jit(solution)/shard_map/ppermute | solution.py:34
  45.3 1.3 %collective-permute-start.17 = (f32[32,1024]{1,0:T(8,128)S(1)}, f32[32,1024]{1,0:T(8,128)S(1)}, u32[]{:S(2)}, u32[]{:S(2)}) collective-permute-start(f32[32,1024]{1,0:T(8,128)S(1)} %collective-permute-done.13.refs_18_), channel_id=1, source_target_pairs={{0,1},{1,0},{2,3},{3,2},{4,5},{5,4},{6,7},{7,6},{8,9},{9,8},{10,11... | collective-permute-start | bytes 393224 | tf_op jit(solution)/shard_map/ppermute | solution.py:34
  57.0 19.2 %collective-permute-start.19 = (f32[64,2560]{1,0:T(8,128)S(1)}, f32[64,2560]{1,0:T(8,128)S(1)}, u32[]{:S(2)}, u32[]{:S(2)}) collective-permute-start(f32[64,2560]{1,0:T(8,128)S(1)} %get-tuple-element.78), channel_id=1, source_target_pairs={{0,16},{16,32},{32,48},{48,0},{64,80},{80,96},{96,112},{112,64},{1... | collective-permute-start | bytes 1966088 | tf_op jit(solution)/shard_map/ppermute | solution.py:43
  59.0 17.2 %collective-permute-start.20 = (f32[64,2560]{1,0:T(8,128)S(1)}, f32[64,2560]{1,0:T(8,128)S(1)}, u32[]{:S(2)}, u32[]{:S(2)}) collective-permute-start(f32[64,2560]{1,0:T(8,128)S(1)} %get-tuple-element.79), channel_id=1, source_target_pairs={{0,48},{16,0},{32,16},{48,32},{64,112},{80,64},{96,80},{112,96},{1... | collective-permute-start | bytes 1966088 | tf_op jit(solution)/shard_map/ppermute | solution.py:43
  61.2 19.4 %collective-permute-start.26 = (f32[128,1536]{1,0:T(8,128)S(1)}, f32[128,1536]{1,0:T(8,128)S(1)}, u32[]{:S(2)}, u32[]{:S(2)}) collective-permute-start(f32[128,1536]{1,0:T(8,128)S(1)} %get-tuple-element.87), channel_id=1, source_target_pairs={{0,64},{16,80},{32,96},{48,112},{64,0},{80,16},{96,32},{112,48},{1... | collective-permute-start | bytes 2359304 | tf_op jit(solution)/shard_map/ppermute | solution.py:43
  76.3 16.1 %collective-permute-start.23 = (f32[32,2560]{1,0:T(8,128)S(1)}, f32[32,2560]{1,0:T(8,128)S(1)}, u32[]{:S(2)}, u32[]{:S(2)}) collective-permute-start(f32[32,2560]{1,0:T(8,128)S(1)} %slice_add_fusion.1), channel_id=1, source_target_pairs={{0,16},{16,32},{32,48},{48,0},{64,80},{80,96},{96,112},{112,64},{1... | collective-permute-start | bytes 983048 | tf_op jit(solution)/shard_map/ppermute | solution.py:43
  77.6 14.8 %collective-permute-start.24 = (f32[32,2560]{1,0:T(8,128)S(1)}, f32[32,2560]{1,0:T(8,128)S(1)}, u32[]{:S(2)}, u32[]{:S(2)}) collective-permute-start(f32[32,2560]{1,0:T(8,128)S(1)} %slice_add_fusion), channel_id=1, source_target_pairs={{0,48},{16,0},{32,16},{48,32},{64,112},{80,64},{96,80},{112,96},{1... | collective-permute-start | bytes 983048 | tf_op jit(solution)/shard_map/ppermute | solution.py:43
  80.7 11.7 %collective-permute-start.28 = (f32[32,1536]{1,0:T(8,128)S(1)}, f32[32,1536]{1,0:T(8,128)S(1)}, u32[]{:S(2)}, u32[]{:S(2)}) collective-permute-start(f32[32,1536]{1,0:T(8,128)S(1)} %get-tuple-element.93), channel_id=1, source_target_pairs={{0,48},{16,0},{32,16},{48,32},{64,112},{80,64},{96,80},{112,96},{1... | collective-permute-start | bytes 589832 | tf_op jit(solution)/shard_map/ppermute | solution.py:43
  82.7 9.8 %collective-permute-start.27 = (f32[32,1536]{1,0:T(8,128)S(1)}, f32[32,1536]{1,0:T(8,128)S(1)}, u32[]{:S(2)}, u32[]{:S(2)}) collective-permute-start(f32[32,1536]{1,0:T(8,128)S(1)} %get-tuple-element.94), channel_id=1, source_target_pairs={{0,16},{16,32},{32,48},{48,0},{64,80},{80,96},{96,112},{112,64},{1... | collective-permute-start | bytes 589832 | tf_op jit(solution)/shard_map/ppermute | solution.py:43
  83.0 3.7 %collective-permute-start.21 = (f32[1,4096]{1,0:T(1,128)S(1)}, f32[1,4096]{1,0:T(1,128)S(1)}, u32[]{:S(2)}, u32[]{:S(2)}) collective-permute-start(f32[1,4096]{1,0:T(1,128)S(1)} %add_add_fusion.2), channel_id=1, source_target_pairs={{0,64},{16,80},{32,96},{48,112},{64,0},{80,16},{96,32},{112,48},{1... | collective-permute-start | bytes 49160 | tf_op jit(solution)/shard_map/ppermute | solution.py:43
  86.8 5.6 %collective-permute-start.22 = (f32[1,4096]{1,0:T(1,128)S(1)}, f32[1,4096]{1,0:T(1,128)S(1)}, u32[]{:S(2)}, u32[]{:S(2)}) collective-permute-start(f32[1,4096]{1,0:T(1,128)S(1)} %add.66), channel_id=1, source_target_pairs={{0,32},{16,48},{32,0},{48,16},{64,96},{80,112},{96,64},{112,80},{1... | collective-permute-start | bytes 49160 | tf_op jit(solution)/shard_map/ppermute | solution.py:43
  92.5 5.9 %collective-permute-start.29 = (f32[16,1536]{1,0:T(8,128)S(1)}, f32[16,1536]{1,0:T(8,128)S(1)}, u32[]{:S(2)}, u32[]{:S(2)}) collective-permute-start(f32[16,1536]{1,0:T(8,128)S(1)} %slice_add_fusion.4), channel_id=1, source_target_pairs={{0,16},{16,32},{32,48},{48,0},{64,80},{80,96},{96,112},{112,64},{1... | collective-permute-start | bytes 294920 | tf_op jit(solution)/shard_map/ppermute | solution.py:43
  93.9 6.0 %collective-permute-start.31 = (f32[1,4096]{1,0:T(1,128)S(1)}, f32[1,4096]{1,0:T(1,128)S(1)}, u32[]{:S(2)}, u32[]{:S(2)}) collective-permute-start(f32[1,4096]{1,0:T(1,128)S(1)} %add.67), channel_id=1, source_target_pairs={{0,16},{16,0},{32,48},{48,32},{64,80},{80,64},{96,112},{112,96},{1... | collective-permute-start | bytes 49160 | tf_op jit(solution)/shard_map/ppermute | solution.py:43
  94.3 8.9 %collective-permute-start.25 = (f32[32,2560]{1,0:T(8,128)S(1)}, f32[32,2560]{1,0:T(8,128)S(1)}, u32[]{:S(2)}, u32[]{:S(2)}) collective-permute-start(f32[32,2560]{1,0:T(8,128)S(1)} %add_add_fusion), channel_id=1, source_target_pairs={{0,64},{16,80},{32,96},{48,112},{64,0},{80,16},{96,32},{112,48},{1... | collective-permute-start | bytes 983048 | tf_op jit(solution)/shard_map/ppermute | solution.py:43
  98.4 4.7 %collective-permute-start.30 = (f32[16,1536]{1,0:T(8,128)S(1)}, f32[16,1536]{1,0:T(8,128)S(1)}, u32[]{:S(2)}, u32[]{:S(2)}) collective-permute-start(f32[16,1536]{1,0:T(8,128)S(1)} %get-tuple-element.92), channel_id=1, source_target_pairs={{0,48},{16,0},{32,16},{48,32},{64,112},{80,64},{96,80},{112,96},{1... | collective-permute-start | bytes 294920 | tf_op jit(solution)/shard_map/ppermute | solution.py:43

commit v4 on v3

--- a/solution.py
+++ b/solution.py
@@ -43,6 +43,10 @@
     return lax.ppermute(x, "layer", pairs)
 
 
+def swap_x_hi(x):
+    return example_permute(x, lambda x_hi, y, core: (1 - x_hi, y, core))
+
+
 def y_up(x):
     return example_permute(x, lambda x_hi, y, core: (x_hi, y + 1, core))
 
@@ -70,10 +74,13 @@
 HEAD = 32
 NEAR = [(0, 0, ROWS, ROWS, 0, 0), (1, 0, ROWS, ROWS, 1, 0), (2, 0, ROWS, ROWS, 0, 1), (3, 0, ROWS, ROWS, 1, 1)]
 FAR = [
-    (4 * core + 2 * x_flip + tail, HEAD * tail, HEAD, HEAD if tail else -1, x_flip, core)
+    block
     for core in range(2)
-    for x_flip in range(2)
-    for tail in range(2)
+    for block in (
+        (3 * core, 0, ROWS, ROWS, 0, core),
+        (3 * core + 1, 0, HEAD, -1, 1, core),
+        (3 * core + 2, HEAD, HEAD, HEAD, 1, core),
+    )
 ]
 
 
@@ -247,19 +254,17 @@
     store = store[0]
 
     own0 = jnp.concatenate([precond[0], queries[0]], axis=0)
-    own1 = example_permute(own0, lambda x_hi, y, core: (1 - x_hi, y, core))
+    own1 = swap_x_hi(own0)
     own1, below0, above0 = tie(own1, y_up(own0), y_down(own0))
     own = (0, with_swapped(own0, own1), NEAR)
     own_hi, own_lo, own_part = part_sizes(where, own, store)
-    below1, above1, *far0, own_part = tie(
-        y_up(own1), y_down(own1), y_up(below0[:HEAD]), y_down(above0[HEAD:]), own_part
-    )
+    below1, above1, far0, own_part = tie(swap_x_hi(below0), y_down(own1), y_up(below0), own_part)
     tail, head = y_up(below1[HEAD:]), y_down(above1[:HEAD])
     below = (-1, with_swapped(below0, below1), NEAR)
     below_hi, below_lo, below_part = part_sizes(where, below, store)
     above = (1, with_swapped(above0, above1), NEAR)
     head, tail, below_part = tie(head, tail, below_part)
-    across = (2, with_swapped(*far0, head, tail), FAR)
+    across = (2, with_swapped(far0, head, tail), FAR)
     rh, rl, *rest = ready_queries(
         where, [own, below, above, across], [(own_hi, own_lo), (below_hi, below_lo), (), ()]
     )
@@ -275,8 +280,8 @@
     last_below, last_above = z_up(up2 + from_below[:32]), z_down(down2 + from_above[:32])
     sizes_sq = sizes_sq + swap_x(sizes_sq)
     home = home + came
-    sizes_sq = sizes_sq + layer_permute(sizes_sq, lambda x_lo, z: (x_lo, z ^ 2))
     sizes_sq, last_below, last_above = tie(sizes_sq, last_below, last_above)
+    sizes_sq = sizes_sq + layer_permute(sizes_sq, lambda x_lo, z: (x_lo, z ^ 1))
     here = mine[:32] + from_above[32:] + last_below
     there = mine[32:] + from_below[32:] + last_above
     first = here + swap_x(there)
@@ -288,7 +293,7 @@
         [home[96:112] + from_above[16:] + last_below, home[112:] + from_below[16:] + last_above], axis=0
     )
 
-    root = jnp.sqrt(sizes_sq + layer_permute(sizes_sq, lambda x_lo, z: (x_lo, z ^ 1)))
+    root = jnp.sqrt(sizes_sq + layer_permute(sizes_sq, lambda x_lo, z: (x_lo, z ^ 2)))
     return jnp.concatenate([first, last], axis=1) / root
 
 

time: 104 us -> 103 us (level)
  waiting for transfers between devices: 26.3 us -> 24 us
  starting transfers between devices: 35.6 us -> 37.1 us
    ppermute x13, waiting for transfers between devices: 15.5 us -> 13.4 us  [layer_permute(): return lax.ppermute(x, 'layer', pairs)]
    ppermute x19 -> x17, starting transfers between devices: 16.5 us -> 17 us  [example_permute(): return lax.ppermute(x, 'example', pairs)]
    ppermute x19 -> x17, waiting for transfers between devices: 10.8 us -> 10.6 us  [example_permute(): return lax.ppermute(x, 'example', pairs)]
  transfers between devices with their start and end apart: 32 -> 30, of which waited for: 12 -> 14; matrix products, arithmetic and copies ran while one was open for 1% -> 1% of each run, Pallas kernels for 22% -> 23%
where the time goes in v4:
time: 103 us
  starting transfers between devices  37.1 us (36%)
  Pallas kernels  33.7 us (33%)
  waiting for transfers between devices  24 us (23%)
  local copies, waits for them, and re-layouts  5.83 us (6%)
  other arithmetic  2.43 us (2%)
    ppermute x13, starting transfers between devices, layer_permute(): return lax.ppermute(x, 'layer', pairs)  20 us
    ppermute x17, starting transfers between devices, example_permute(): return lax.ppermute(x, 'example', pairs)  17 us
    ppermute x13, waiting for transfers between devices, layer_permute(): return lax.ppermute(x, 'layer', pairs)  13.4 us
    pallas_call x2, Pallas kernels, part_sizes(): pl.pallas_call(functools.partial(part_kernel, blocks, y_shift, len(buffer...  12.3 us
    pallas_call x1, Pallas kernels, rest_sizes(): pl.pallas_call(functools.partial(rest_kernel, y_shifts), in_specs=[SMEM]...  10.9 us
    ppermute x17, waiting for transfers between devices, example_permute(): return lax.ppermute(x, 'example', pairs)  10.6 us
    pallas_call x2, Pallas kernels, raw_scores(): pl.pallas_call(functools.partial(raw_kernel, first, runs), in_specs=[VMEM...  7.36 us
    unnamed x4, local copies, waits for them, and re-layouts  5.77 us
  transfers between devices with their start and end apart: 30, of which 14 were waited for; matrix products, arithmetic and copies ran while one was open for 1% of the time, Pallas kernels for 23%

profile of v4, /device:TPU:0, one launch (start us, length us, event | category | flops | bytes accessed | tf_op | source)
XLA Modules:
  0.0 103.1 jit_solution(13739247453844592577)
XLA Ops:
  0.0 1.0 pad_maximum_fusion.refs_0_
  1.0 3.2 %collective-permute-start.2 = (f32[80,1024]{1,0:T(8,128)S(1)}, f32[80,1024]{1,0:T(8,128)S(1)}, u32[]{:S(2)}, u32[]{:S(2)}) collective-permute-start(f32[80,1024]{1,0:T(8,128)S(1)} %pad_maximum_fusion.refs_0_), channel_id=1, source_target_pairs={{0,6},{1,7},{2,0},{3,1},{4,2},{5,3},{6,4},{7,5},{8,14},{9,15},{10,... | collective-permute-start | bytes 983048 | tf_op jit(solution)/shard_map/ppermute | solution.py:34
  4.2 0.0 collective-permute-start.1
  4.2 3.0 %collective-permute-start = (f32[80,1024]{1,0:T(8,128)S(1)}, f32[80,1024]{1,0:T(8,128)S(1)}, u32[]{:S(2)}, u32[]{:S(2)}) collective-permute-start(f32[80,1024]{1,0:T(8,128)S(1)} %pad_maximum_fusion.refs_0_), channel_id=1, source_target_pairs={{0,8},{1,9},{2,10},{3,11},{4,12},{5,13},{6,14},{7,15},{8,0},{9,1},... | collective-permute-start | bytes 983048 | tf_op jit(solution)/shard_map/ppermute | solution.py:34
  7.2 0.0 collective-permute-start.3
  7.2 3.9 %collective-permute-done.2.refs_12_ = f32[80,1024]{1,0:T(8,128)S(1)} collective-permute-done((f32[80,1024]{1,0:T(8,128)S(1)}, f32[80,1024]{1,0:T(8,128)S(1)}, u32[]{:S(2)}, u32[]{:S(2)}) %collective-permute-start.2) | collective-permute-done | bytes 327712 | tf_op jit(solution)/shard_map/ppermute | solution.py:34
  11.2 3.4 %collective-permute-done.1.refs_0_.refs_6_ = f32[80,1024]{1,0:T(8,128)S(1)} collective-permute-done((f32[80,1024]{1,0:T(8,128)S(1)}, f32[80,1024]{1,0:T(8,128)S(1)}, u32[]{:S(2)}, u32[]{:S(2)}) %collective-permute-start.1) | collective-permute-done | bytes 327712 | tf_op jit(solution)/shard_map/ppermute | solution.py:34
  14.6 0.3 collective-permute-done.refs_1_
  14.9 0.0 collective-permute-start.4
  14.9 0.1 pad_add_fusion.where_ref
  14.9 3.0 %collective-permute-start.6 = (f32[80,1024]{1,0:T(8,128)S(1)}, f32[80,1024]{1,0:T(8,128)S(1)}, u32[]{:S(2)}, u32[]{:S(2)}) collective-permute-start(f32[80,1024]{1,0:T(8,128)S(1)} %collective-permute-done.refs_1_), channel_id=1, source_target_pairs={{0,6},{1,7},{2,0},{3,1},{4,2},{5,3},{6,4},{7,5},{8,14},{9,15},{10,... | collective-permute-start | bytes 983048 | tf_op jit(solution)/shard_map/ppermute | solution.py:34
  17.9 0.2 collective-permute-start.8
  18.1 3.0 %collective-permute-start.5 = (f32[80,1024]{1,0:T(8,128)S(1)}, f32[80,1024]{1,0:T(8,128)S(1)}, u32[]{:S(2)}, u32[]{:S(2)}) collective-permute-start(f32[80,1024]{1,0:T(8,128)S(1)} %collective-permute-done.1.refs_0_.refs_6_), channel_id=1, source_target_pairs={{0,8},{1,9},{2,10},{3,11},{4,12},{5,13},{6,14},{7,15},{8,0},{9,1},... | collective-permute-start | bytes 983048 | tf_op jit(solution)/shard_map/ppermute | solution.py:34
  21.2 5.8 %copy-done = f32[1,4096,1024]{2,1,0:T(8,128)S(1)} copy-done((f32[1,4096,1024]{2,1,0:T(8,128)S(1)}, f32[1,4096,1024]{2,1,0:T(8,128)}, u32[]{:S(2)}) %copy-start) | copy-done | bytes 16777240
  26.9 6.2 %shard_map.37 = (bf16[256,1024]{1,0:T(8,128)(2,1)S(1)}, bf16[256,1024]{1,0:T(8,128)(2,1)S(1)}, f32[1,4096]{1,0:T(1,128)S(1)}) custom-call(s32[3]{0:T(128)S(1)} %pad_add_fusion.where_ref, f32[80,1024]{1,0:T(8,128)S(1)} %pad_maximum_fusion.refs_0_, f32[80,1024]{1,0:T(8,128)S(1)} %collective-permute-done.refs_1_, ...), custom_call_target="tpu_custom_call" | custom-call | flops 8589934592 | bytes 16777216 | tf_op jit(solution)/shard_map/pallas_call | solution.py:128
  33.2 0.0 collective-permute-done.6.refs_13_
  33.2 0.0 collective-permute-done.7.refs_16_
  33.2 0.1 collective-permute-start.9
  33.3 0.5 collective-permute-start.10
  33.8 0.2 collective-permute-start.11
  34.0 3.1 %collective-permute-start.12 = (f32[32,1024]{1,0:T(8,128)S(1)}, f32[32,1024]{1,0:T(8,128)S(1)}, u32[]{:S(2)}, u32[]{:S(2)}) collective-permute-start(f32[32,1024]{1,0:T(8,128)S(1)} %slice.54), channel_id=1, source_target_pairs={{0,6},{1,7},{2,0},{3,1},{4,2},{5,3},{6,4},{7,5},{8,14},{9,15},{10,... | collective-permute-start | bytes 393224 | tf_op jit(solution)/shard_map/ppermute | solution.py:34
  37.1 0.0 collective-permute-start.13
  37.1 0.0 collective-permute-done.9.refs_3_.refs_9_
  37.1 0.2 collective-permute-start.14
  37.4 6.1 %shard_map.38 = (bf16[256,1024]{1,0:T(8,128)(2,1)S(1)}, bf16[256,1024]{1,0:T(8,128)(2,1)S(1)}, f32[1,4096]{1,0:T(1,128)S(1)}) custom-call(s32[3]{0:T(128)S(1)} %pad_add_fusion.where_ref, f32[80,1024]{1,0:T(8,128)S(1)} %collective-permute-done.1.refs_0_.refs_6_, f32[80,1024]{1,0:T(8,128)S(1)} %collective-permute-done.5.refs_1_.refs_7_, ...), custom_call_target="tpu_custom_call" | custom-call | flops 8589934592 | bytes 16777216 | tf_op jit(solution)/shard_map/pallas_call | solution.py:128
  43.5 0.0 collective-permute-done.12.refs_17_
  43.5 1.8 %collective-permute-done.13.refs_18_ = f32[48,1024]{1,0:T(8,128)S(1)} collective-permute-done((f32[48,1024]{1,0:T(8,128)S(1)}, f32[48,1024]{1,0:T(8,128)S(1)}, u32[]{:S(2)}, u32[]{:S(2)}) %collective-permute-start.13) | collective-permute-done | bytes 196640 | tf_op jit(solution)/shard_map/ppermute | solution.py:34
  45.3 0.0 collective-permute-start.16
  45.3 0.5 collective-permute-start.15
  45.8 0.0 collective-permute-done.10.refs_14_
  45.8 0.0 collective-permute-done.14.refs_19_
  45.8 0.0 collective-permute-done.11.refs_15_
  45.8 1.1 %collective-permute-done.15.refs_20_ = f32[32,1024]{1,0:T(8,128)S(1)} collective-permute-done((f32[32,1024]{1,0:T(8,128)S(1)}, f32[32,1024]{1,0:T(8,128)S(1)}, u32[]{:S(2)}, u32[]{:S(2)}) %collective-permute-start.15) | collective-permute-done | bytes 131104 | tf_op jit(solution)/shard_map/ppermute | solution.py:34
  46.9 3.1 %shard_map.39 = (bf16[256,1024]{1,0:T(8,128)(2,1)S(1)}, bf16[256,1024]{1,0:T(8,128)(2,1)S(1)}, bf16[256,1024]{1,0:T(8,128)(2,1)S(1)}, bf16[256,1024]{1,0:T(8,128...) custom-call(s32[3]{0:T(128)S(1)} %pad_add_fusion.where_ref, ...), custom_call_target="tpu_custom_call" | custom-call | flops 1610612736 | bytes 1048576 | tf_op jit(solution)/shard_map/pallas_call | solution.py:204
  50.0 4.5 %shard_map.40 = (f32[64,2560]{1,0:T(8,128)S(1)}, f32[64,2560]{1,0:T(8,128)S(1)}, f32[32,2560]{1,0:T(8,128)S(1)}, f32[32,2560]{1,0:T(8,128)S(1)}, f32[64,2560]{1,0:T(8,128)S(1)}) custom-call(bf16[256,1024]{1,0:T(8,128)(2,1)S(1)} %get-tuple-element.70.rh_ref, bf16[256,1024]{1,0:T(8,128)(2,1)S(1)} %get-tuple-element.62.rl_ref, f32[4096,1024]{1,0:T(8,128)S(1)} %bitcast.9), custom_call_target="tpu_custom_call" | custom-call | flops 5368709120 | bytes 13107200 | tf_op jit(solution)/shard_map/pallas_call | solution.py:239
  54.5 2.9 %shard_map.41 = (f32[128,1536]{1,0:T(8,128)S(1)}, f32[128,1536]{1,0:T(8,128)S(1)}) custom-call(bf16[256,1024]{1,0:T(8,128)(2,1)S(1)} %get-tuple-element.70.rh_ref, bf16[256,1024]{1,0:T(8,128)(2,1)S(1)} %get-tuple-element.62.rl_ref, f32[4096,1024]{1,0:T(8,128)S(1)} %bitcast.10), custom_call_target="tpu_custom_call" | custom-call | flops 3221225472 | bytes 7864320 | tf_op jit(solution)/shard_map/pallas_call | solution.py:239
  57.4 2.0 %collective-permute-start.17 = (f32[64,2560]{1,0:T(8,128)S(1)}, f32[64,2560]{1,0:T(8,128)S(1)}, u32[]{:S(2)}, u32[]{:S(2)}) collective-permute-start(f32[64,2560]{1,0:T(8,128)S(1)} %get-tuple-element.76), channel_id=1, source_target_pairs={{0,16},{16,32},{32,48},{48,0},{64,80},{80,96},{96,112},{112,64},{1... | collective-permute-start | bytes 1966088 | tf_op jit(solution)/shard_map/ppermute | solution.py:43
  59.4 2.2 %collective-permute-start.18 = (f32[64,2560]{1,0:T(8,128)S(1)}, f32[64,2560]{1,0:T(8,128)S(1)}, u32[]{:S(2)}, u32[]{:S(2)}) collective-permute-start(f32[64,2560]{1,0:T(8,128)S(1)} %get-tuple-element.77), channel_id=1, source_target_pairs={{0,48},{16,0},{32,16},{48,32},{64,112},{80,64},{96,80},{112,96},{1... | collective-permute-start | bytes 1966088 | tf_op jit(solution)/shard_map/ppermute | solution.py:43
  61.5 0.6 collective-permute-start.23
  62.2 10.9 %shard_map.42 = f32[1,4096]{1,0:T(1,128)S(1)} custom-call(s32[3]{0:T(128)S(1)} %pad_add_fusion.where_ref, bf16[256,1024]{1,0:T(8,128)(2,1)S(1)} %get-tuple-element.72.refs_0_, bf16[256,1024]{1,0:T(8,128)(2,1)S(1)} %get-tuple-element.73.refs_1_, bf16[256,1024]{1,0:T(8,128)(2,1)S(1)} %get-tuple-element.74.refs_2_, ...), custom_call_target="tpu_custom_call" | custom-call | flops 1 | bytes 1 | tf_op jit(solution)/shard_map/pallas_call | solution.py:148
  73.1 3.5 %collective-permute-done.17 = f32[64,2560]{1,0:T(8,128)S(1)} collective-permute-done((f32[64,2560]{1,0:T(8,128)S(1)}, f32[64,2560]{1,0:T(8,128)S(1)}, u32[]{:S(2)}, u32[]{:S(2)}) %collective-permute-start.17) | collective-permute-done | bytes 655392 | tf_op jit(solution)/shard_map/ppermute | solution.py:43
  76.6 1.3 %collective-permute-start.20 = (f32[32,2560]{1,0:T(8,128)S(1)}, f32[32,2560]{1,0:T(8,128)S(1)}, u32[]{:S(2)}, u32[]{:S(2)}) collective-permute-start(f32[32,2560]{1,0:T(8,128)S(1)} %slice_add_fusion.1), channel_id=1, source_target_pairs={{0,16},{16,32},{32,48},{48,0},{64,80},{80,96},{96,112},{112,64},{1... | collective-permute-start | bytes 983048 | tf_op jit(solution)/shard_map/ppermute | solution.py:43
  78.0 0.1 slice_add_fusion
  78.0 2.0 %collective-permute-start.21 = (f32[32,2560]{1,0:T(8,128)S(1)}, f32[32,2560]{1,0:T(8,128)S(1)}, u32[]{:S(2)}, u32[]{:S(2)}) collective-permute-start(f32[32,2560]{1,0:T(8,128)S(1)} %slice_add_fusion), channel_id=1, source_target_pairs={{0,48},{16,0},{32,16},{48,32},{64,112},{80,64},{96,80},{112,96},{1... | collective-permute-start | bytes 983048 | tf_op jit(solution)/shard_map/ppermute | solution.py:43
  80.0 0.9 collective-permute-done.23
  80.9 0.1 add.73
  81.1 2.0 %collective-permute-start.25 = (f32[32,1536]{1,0:T(8,128)S(1)}, f32[32,1536]{1,0:T(8,128)S(1)}, u32[]{:S(2)}, u32[]{:S(2)}) collective-permute-start(f32[32,1536]{1,0:T(8,128)S(1)} %get-tuple-element.91), channel_id=1, source_target_pairs={{0,48},{16,0},{32,16},{48,32},{64,112},{80,64},{96,80},{112,96},{1... | collective-permute-start | bytes 589832 | tf_op jit(solution)/shard_map/ppermute | solution.py:43
  83.0 0.4 collective-permute-start.24
  83.4 0.6 collective-permute-start.19
  84.0 3.1 %collective-permute-done.19 = f32[1,4096]{1,0:T(1,128)S(1)} collective-permute-done((f32[1,4096]{1,0:T(1,128)S(1)}, f32[1,4096]{1,0:T(1,128)S(1)}, u32[]{:S(2)}, u32[]{:S(2)}) %collective-permute-start.19) | collective-permute-done | bytes 16416 | tf_op jit(solution)/shard_map/ppermute | solution.py:43
  87.1 1.4 %collective-permute-done.20 = f32[32,2560]{1,0:T(8,128)S(1)} collective-permute-done((f32[32,2560]{1,0:T(8,128)S(1)}, f32[32,2560]{1,0:T(8,128)S(1)}, u32[]{:S(2)}, u32[]{:S(2)}) %collective-permute-start.20) | collective-permute-done | bytes 327712 | tf_op jit(solution)/shard_map/ppermute | solution.py:43
  88.5 0.1 collective-permute-done.21
  88.6 1.7 %collective-permute-start.28 = (f32[1,4096]{1,0:T(1,128)S(1)}, f32[1,4096]{1,0:T(1,128)S(1)}, u32[]{:S(2)}, u32[]{:S(2)}) collective-permute-start(f32[1,4096]{1,0:T(1,128)S(1)} %add.66), channel_id=1, source_target_pairs={{0,16},{16,0},{32,48},{48,32},{64,80},{80,64},{96,112},{112,96},{1... | collective-permute-start | bytes 49160 | tf_op jit(solution)/shard_map/ppermute | solution.py:43
  90.4 0.6 collective-permute-done.25
  90.9 0.5 collective-permute-done.24
  91.5 1.1 %collective-permute-start.26 = (f32[16,1536]{1,0:T(8,128)S(1)}, f32[16,1536]{1,0:T(8,128)S(1)}, u32[]{:S(2)}, u32[]{:S(2)}) collective-permute-start(f32[16,1536]{1,0:T(8,128)S(1)} %slice_add_fusion.4), channel_id=1, source_target_pairs={{0,16},{16,32},{32,48},{48,0},{64,80},{80,96},{96,112},{112,64},{1... | collective-permute-start | bytes 294920 | tf_op jit(solution)/shard_map/ppermute | solution.py:43
  92.6 0.1 add_add_fusion
  92.6 0.7 collective-permute-start.22
  93.3 3.6 %collective-permute-start.29 = (f32[1,4096]{1,0:T(1,128)S(1)}, f32[1,4096]{1,0:T(1,128)S(1)}, u32[]{:S(2)}, u32[]{:S(2)}) collective-permute-start(f32[1,4096]{1,0:T(1,128)S(1)} %add.80), channel_id=1, source_target_pairs={{0,32},{16,48},{32,0},{48,16},{64,96},{80,112},{96,64},{112,80},{1... | collective-permute-start | bytes 49160 | tf_op jit(solution)/shard_map/ppermute | solution.py:43
  96.9 0.5 collective-permute-done.26
  97.5 1.9 %collective-permute-start.27 = (f32[16,1536]{1,0:T(8,128)S(1)}, f32[16,1536]{1,0:T(8,128)S(1)}, u32[]{:S(2)}, u32[]{:S(2)}) collective-permute-start(f32[16,1536]{1,0:T(8,128)S(1)} %get-tuple-element.90), channel_id=1, source_target_pairs={{0,48},{16,0},{32,16},{48,32},{64,112},{80,64},{96,80},{112,96},{1... | collective-permute-start | bytes 294920 | tf_op jit(solution)/shard_map/ppermute | solution.py:43
  99.4 2.8 %collective-permute-done.27 = f32[16,1536]{1,0:T(8,128)S(1)} collective-permute-done((f32[16,1536]{1,0:T(8,128)S(1)}, f32[16,1536]{1,0:T(8,128)S(1)}, u32[]{:S(2)}, u32[]{:S(2)}) %collective-permute-start.27) | collective-permute-done | bytes 98336 | tf_op jit(solution)/shard_map/ppermute | solution.py:43
  102.2 0.1 add_add_fusion.1
  102.3 0.8 maximum_divide_fusion
  (24 shorter events, 0.3 us)
Async XLA Ops:
  1.0 10.1 %collective-permute-start.2 = (f32[80,1024]{1,0:T(8,128)S(1)}, f32[80,1024]{1,0:T(8,128)S(1)}, u32[]{:S(2)}, u32[]{:S(2)}) collective-permute-start(f32[80,1024]{1,0:T(8,128)S(1)} %pad_maximum_fusion.refs_0_), channel_id=1, source_target_pairs={{0,6},{1,7},{2,0},{3,1},{4,2},{5,3},{6,4},{7,5},{8,14},{9,15},{10,... | collective-permute-start | bytes 983048 | tf_op jit(solution)/shard_map/ppermute | solution.py:34
  4.2 10.4 %collective-permute-start.1 = (f32[80,1024]{1,0:T(8,128)S(1)}, f32[80,1024]{1,0:T(8,128)S(1)}, u32[]{:S(2)}, u32[]{:S(2)}) collective-permute-start(f32[80,1024]{1,0:T(8,128)S(1)} %pad_maximum_fusion.refs_0_), channel_id=1, source_target_pairs={{0,2},{1,3},{2,4},{3,5},{4,6},{5,7},{6,0},{7,1},{8,10},{9,11},{10,... | collective-permute-start | bytes 983048 | tf_op jit(solution)/shard_map/ppermute | solution.py:34
  4.2 10.7 %collective-permute-start = (f32[80,1024]{1,0:T(8,128)S(1)}, f32[80,1024]{1,0:T(8,128)S(1)}, u32[]{:S(2)}, u32[]{:S(2)}) collective-permute-start(f32[80,1024]{1,0:T(8,128)S(1)} %pad_maximum_fusion.refs_0_), channel_id=1, source_target_pairs={{0,8},{1,9},{2,10},{3,11},{4,12},{5,13},{6,14},{7,15},{8,0},{9,1},... | collective-permute-start | bytes 983048 | tf_op jit(solution)/shard_map/ppermute | solution.py:34
  7.2 10.9 %collective-permute-start.3 = (f32[80,1024]{1,0:T(8,128)S(1)}, f32[80,1024]{1,0:T(8,128)S(1)}, u32[]{:S(2)}, u32[]{:S(2)}) collective-permute-start(f32[80,1024]{1,0:T(8,128)S(1)} %pad_maximum_fusion.refs_0_), channel_id=1, source_target_pairs={{0,1},{1,0},{2,3},{3,2},{4,5},{5,4},{6,7},{7,6},{8,9},{9,8},{10,11... | collective-permute-start | bytes 983048 | tf_op jit(solution)/shard_map/ppermute | solution.py:34
  14.9 6.3 %collective-permute-start.4 = (f32[80,1024]{1,0:T(8,128)S(1)}, f32[80,1024]{1,0:T(8,128)S(1)}, u32[]{:S(2)}, u32[]{:S(2)}) collective-permute-start(f32[80,1024]{1,0:T(8,128)S(1)} %collective-permute-done.refs_1_), channel_id=1, source_target_pairs={{0,1},{1,0},{2,3},{3,2},{4,5},{5,4},{6,7},{7,6},{8,9},{9,8},{10,11... | collective-permute-start | bytes 983048 | tf_op jit(solution)/shard_map/ppermute | solution.py:34
  14.9 18.2 %collective-permute-start.6 = (f32[80,1024]{1,0:T(8,128)S(1)}, f32[80,1024]{1,0:T(8,128)S(1)}, u32[]{:S(2)}, u32[]{:S(2)}) collective-permute-start(f32[80,1024]{1,0:T(8,128)S(1)} %collective-permute-done.refs_1_), channel_id=1, source_target_pairs={{0,6},{1,7},{2,0},{3,1},{4,2},{5,3},{6,4},{7,5},{8,14},{9,15},{10,... | collective-permute-start | bytes 983048 | tf_op jit(solution)/shard_map/ppermute | solution.py:34
  17.9 19.2 %collective-permute-start.8 = (f32[80,1024]{1,0:T(8,128)S(1)}, f32[80,1024]{1,0:T(8,128)S(1)}, u32[]{:S(2)}, u32[]{:S(2)}) collective-permute-start(f32[80,1024]{1,0:T(8,128)S(1)} %collective-permute-done.1.refs_0_.refs_6_), channel_id=1, source_target_pairs={{0,1},{1,0},{2,3},{3,2},{4,5},{5,4},{6,7},{7,6},{8,9},{9,8},{10,11... | collective-permute-start | bytes 983048 | tf_op jit(solution)/shard_map/ppermute | solution.py:34
  18.1 15.0 %collective-permute-start.7 = (f32[80,1024]{1,0:T(8,128)S(1)}, f32[80,1024]{1,0:T(8,128)S(1)}, u32[]{:S(2)}, u32[]{:S(2)}) collective-permute-start(f32[80,1024]{1,0:T(8,128)S(1)} %collective-permute-done.1.refs_0_.refs_6_), channel_id=1, source_target_pairs={{0,2},{1,3},{2,4},{3,5},{4,6},{5,7},{6,0},{7,1},{8,10},{9,11},{10,... | collective-permute-start | bytes 983048 | tf_op jit(solution)/shard_map/ppermute | solution.py:34
  18.1 15.0 %collective-permute-start.5 = (f32[80,1024]{1,0:T(8,128)S(1)}, f32[80,1024]{1,0:T(8,128)S(1)}, u32[]{:S(2)}, u32[]{:S(2)}) collective-permute-start(f32[80,1024]{1,0:T(8,128)S(1)} %collective-permute-done.1.refs_0_.refs_6_), channel_id=1, source_target_pairs={{0,8},{1,9},{2,10},{3,11},{4,12},{5,13},{6,14},{7,15},{8,0},{9,1},... | collective-permute-start | bytes 983048 | tf_op jit(solution)/shard_map/ppermute | solution.py:34
  21.2 5.8 %copy-start = (f32[1,4096,1024]{2,1,0:T(8,128)S(1)}, f32[1,4096,1024]{2,1,0:T(8,128)}, u32[]{:S(2)}) copy-start(f32[1,4096,1024]{2,1,0:T(8,128)} %param.5) | copy-start | bytes 50331652
  26.9 10.4 %copy-start.1 = (f32[1,4096,1024]{2,1,0:T(8,128)S(1)}, f32[1,4096,1024]{2,1,0:T(8,128)}, u32[]{:S(2)}) copy-start(f32[1,4096,1024]{2,1,0:T(8,128)} %param.5) | copy-start | bytes 50331652
  33.2 3.9 %collective-permute-start.9 = (f32[80,1024]{1,0:T(8,128)S(1)}, f32[80,1024]{1,0:T(8,128)S(1)}, u32[]{:S(2)}, u32[]{:S(2)}) collective-permute-start(f32[80,1024]{1,0:T(8,128)S(1)} %collective-permute-done.5.refs_1_.refs_7_), channel_id=1, source_target_pairs={{0,1},{1,0},{2,3},{3,2},{4,5},{5,4},{6,7},{7,6},{8,9},{9,8},{10,11... | collective-permute-start | bytes 983048 | tf_op jit(solution)/shard_map/ppermute | solution.py:34
  33.3 12.5 %collective-permute-start.10 = (f32[80,1024]{1,0:T(8,128)S(1)}, f32[80,1024]{1,0:T(8,128)S(1)}, u32[]{:S(2)}, u32[]{:S(2)}) collective-permute-start(f32[80,1024]{1,0:T(8,128)S(1)} %collective-permute-done.2.refs_12_), channel_id=1, source_target_pairs={{0,1},{1,0},{2,3},{3,2},{4,5},{5,4},{6,7},{7,6},{8,9},{9,8},{10,11... | collective-permute-start | bytes 983048 | tf_op jit(solution)/shard_map/ppermute | solution.py:34
  33.8 12.0 %collective-permute-start.11 = (f32[80,1024]{1,0:T(8,128)S(1)}, f32[80,1024]{1,0:T(8,128)S(1)}, u32[]{:S(2)}, u32[]{:S(2)}) collective-permute-start(f32[80,1024]{1,0:T(8,128)S(1)} %collective-permute-done.6.refs_13_), channel_id=1, source_target_pairs={{0,1},{1,0},{2,3},{3,2},{4,5},{5,4},{6,7},{7,6},{8,9},{9,8},{10,11... | collective-permute-start | bytes 983048 | tf_op jit(solution)/shard_map/ppermute | solution.py:34
  34.0 9.5 %collective-permute-start.12 = (f32[32,1024]{1,0:T(8,128)S(1)}, f32[32,1024]{1,0:T(8,128)S(1)}, u32[]{:S(2)}, u32[]{:S(2)}) collective-permute-start(f32[32,1024]{1,0:T(8,128)S(1)} %slice.54), channel_id=1, source_target_pairs={{0,6},{1,7},{2,0},{3,1},{4,2},{5,3},{6,4},{7,5},{8,14},{9,15},{10,... | collective-permute-start | bytes 393224 | tf_op jit(solution)/shard_map/ppermute | solution.py:34
  37.1 8.2 %collective-permute-start.13 = (f32[48,1024]{1,0:T(8,128)S(1)}, f32[48,1024]{1,0:T(8,128)S(1)}, u32[]{:S(2)}, u32[]{:S(2)}) collective-permute-start(f32[48,1024]{1,0:T(8,128)S(1)} %slice.55), channel_id=1, source_target_pairs={{0,2},{1,3},{2,4},{3,5},{4,6},{5,7},{6,0},{7,1},{8,10},{9,11},{10,... | collective-permute-start | bytes 589832 | tf_op jit(solution)/shard_map/ppermute | solution.py:34
  37.1 8.7 %collective-permute-start.14 = (f32[80,1024]{1,0:T(8,128)S(1)}, f32[80,1024]{1,0:T(8,128)S(1)}, u32[]{:S(2)}, u32[]{:S(2)}) collective-permute-start(f32[80,1024]{1,0:T(8,128)S(1)} %collective-permute-done.7.refs_16_), channel_id=1, source_target_pairs={{0,1},{1,0},{2,3},{3,2},{4,5},{5,4},{6,7},{7,6},{8,9},{9,8},{10,11... | collective-permute-start | bytes 983048 | tf_op jit(solution)/shard_map/ppermute | solution.py:34
  45.3 1.6 %collective-permute-start.16 = (f32[48,1024]{1,0:T(8,128)S(1)}, f32[48,1024]{1,0:T(8,128)S(1)}, u32[]{:S(2)}, u32[]{:S(2)}) collective-permute-start(f32[48,1024]{1,0:T(8,128)S(1)} %collective-permute-done.13.refs_18_), channel_id=1, source_target_pairs={{0,1},{1,0},{2,3},{3,2},{4,5},{5,4},{6,7},{7,6},{8,9},{9,8},{10,11... | collective-permute-start | bytes 589832 | tf_op jit(solution)/shard_map/ppermute | solution.py:34
  45.3 1.6 %collective-permute-start.15 = (f32[32,1024]{1,0:T(8,128)S(1)}, f32[32,1024]{1,0:T(8,128)S(1)}, u32[]{:S(2)}, u32[]{:S(2)}) collective-permute-start(f32[32,1024]{1,0:T(8,128)S(1)} %collective-permute-done.12.refs_17_), channel_id=1, source_target_pairs={{0,1},{1,0},{2,3},{3,2},{4,5},{5,4},{6,7},{7,6},{8,9},{9,8},{10,11... | collective-permute-start | bytes 393224 | tf_op jit(solution)/shard_map/ppermute | solution.py:34
  57.4 19.2 %collective-permute-start.17 = (f32[64,2560]{1,0:T(8,128)S(1)}, f32[64,2560]{1,0:T(8,128)S(1)}, u32[]{:S(2)}, u32[]{:S(2)}) collective-permute-start(f32[64,2560]{1,0:T(8,128)S(1)} %get-tuple-element.76), channel_id=1, source_target_pairs={{0,16},{16,32},{32,48},{48,0},{64,80},{80,96},{96,112},{112,64},{1... | collective-permute-start | bytes 1966088 | tf_op jit(solution)/shard_map/ppermute | solution.py:43
  59.4 17.2 %collective-permute-start.18 = (f32[64,2560]{1,0:T(8,128)S(1)}, f32[64,2560]{1,0:T(8,128)S(1)}, u32[]{:S(2)}, u32[]{:S(2)}) collective-permute-start(f32[64,2560]{1,0:T(8,128)S(1)} %get-tuple-element.77), channel_id=1, source_target_pairs={{0,48},{16,0},{32,16},{48,32},{64,112},{80,64},{96,80},{112,96},{1... | collective-permute-start | bytes 1966088 | tf_op jit(solution)/shard_map/ppermute | solution.py:43
  61.5 19.4 %collective-permute-start.23 = (f32[128,1536]{1,0:T(8,128)S(1)}, f32[128,1536]{1,0:T(8,128)S(1)}, u32[]{:S(2)}, u32[]{:S(2)}) collective-permute-start(f32[128,1536]{1,0:T(8,128)S(1)} %get-tuple-element.85), channel_id=1, source_target_pairs={{0,64},{16,80},{32,96},{48,112},{64,0},{80,16},{96,32},{112,48},{1... | collective-permute-start | bytes 2359304 | tf_op jit(solution)/shard_map/ppermute | solution.py:43
  76.6 11.9 %collective-permute-start.20 = (f32[32,2560]{1,0:T(8,128)S(1)}, f32[32,2560]{1,0:T(8,128)S(1)}, u32[]{:S(2)}, u32[]{:S(2)}) collective-permute-start(f32[32,2560]{1,0:T(8,128)S(1)} %slice_add_fusion.1), channel_id=1, source_target_pairs={{0,16},{16,32},{32,48},{48,0},{64,80},{80,96},{96,112},{112,64},{1... | collective-permute-start | bytes 983048 | tf_op jit(solution)/shard_map/ppermute | solution.py:43
  78.0 10.6 %collective-permute-start.21 = (f32[32,2560]{1,0:T(8,128)S(1)}, f32[32,2560]{1,0:T(8,128)S(1)}, u32[]{:S(2)}, u32[]{:S(2)}) collective-permute-start(f32[32,2560]{1,0:T(8,128)S(1)} %slice_add_fusion), channel_id=1, source_target_pairs={{0,48},{16,0},{32,16},{48,32},{64,112},{80,64},{96,80},{112,96},{1... | collective-permute-start | bytes 983048 | tf_op jit(solution)/shard_map/ppermute | solution.py:43
  81.1 9.8 %collective-permute-start.25 = (f32[32,1536]{1,0:T(8,128)S(1)}, f32[32,1536]{1,0:T(8,128)S(1)}, u32[]{:S(2)}, u32[]{:S(2)}) collective-permute-start(f32[32,1536]{1,0:T(8,128)S(1)} %get-tuple-element.91), channel_id=1, source_target_pairs={{0,48},{16,0},{32,16},{48,32},{64,112},{80,64},{96,80},{112,96},{1... | collective-permute-start | bytes 589832 | tf_op jit(solution)/shard_map/ppermute | solution.py:43
  83.0 8.4 %collective-permute-start.24 = (f32[32,1536]{1,0:T(8,128)S(1)}, f32[32,1536]{1,0:T(8,128)S(1)}, u32[]{:S(2)}, u32[]{:S(2)}) collective-permute-start(f32[32,1536]{1,0:T(8,128)S(1)} %get-tuple-element.92), channel_id=1, source_target_pairs={{0,16},{16,32},{32,48},{48,0},{64,80},{80,96},{96,112},{112,64},{1... | collective-permute-start | bytes 589832 | tf_op jit(solution)/shard_map/ppermute | solution.py:43
  83.4 3.7 %collective-permute-start.19 = (f32[1,4096]{1,0:T(1,128)S(1)}, f32[1,4096]{1,0:T(1,128)S(1)}, u32[]{:S(2)}, u32[]{:S(2)}) collective-permute-start(f32[1,4096]{1,0:T(1,128)S(1)} %add_add_fusion.2), channel_id=1, source_target_pairs={{0,64},{16,80},{32,96},{48,112},{64,0},{80,16},{96,32},{112,48},{1... | collective-permute-start | bytes 49160 | tf_op jit(solution)/shard_map/ppermute | solution.py:43
  88.6 4.7 %collective-permute-start.28 = (f32[1,4096]{1,0:T(1,128)S(1)}, f32[1,4096]{1,0:T(1,128)S(1)}, u32[]{:S(2)}, u32[]{:S(2)}) collective-permute-start(f32[1,4096]{1,0:T(1,128)S(1)} %add.66), channel_id=1, source_target_pairs={{0,16},{16,0},{32,48},{48,32},{64,80},{80,64},{96,112},{112,96},{1... | collective-permute-start | bytes 49160 | tf_op jit(solution)/shard_map/ppermute | solution.py:43
  91.5 6.0 %collective-permute-start.26 = (f32[16,1536]{1,0:T(8,128)S(1)}, f32[16,1536]{1,0:T(8,128)S(1)}, u32[]{:S(2)}, u32[]{:S(2)}) collective-permute-start(f32[16,1536]{1,0:T(8,128)S(1)} %slice_add_fusion.4), channel_id=1, source_target_pairs={{0,16},{16,32},{32,48},{48,0},{64,80},{80,96},{96,112},{112,64},{1... | collective-permute-start | bytes 294920 | tf_op jit(solution)/shard_map/ppermute | solution.py:43
  92.6 9.6 %collective-permute-start.22 = (f32[32,2560]{1,0:T(8,128)S(1)}, f32[32,2560]{1,0:T(8,128)S(1)}, u32[]{:S(2)}, u32[]{:S(2)}) collective-permute-start(f32[32,2560]{1,0:T(8,128)S(1)} %add_add_fusion), channel_id=1, source_target_pairs={{0,64},{16,80},{32,96},{48,112},{64,0},{80,16},{96,32},{112,48},{1... | collective-permute-start | bytes 983048 | tf_op jit(solution)/shard_map/ppermute | solution.py:43
  93.3 6.0 %collective-permute-start.29 = (f32[1,4096]{1,0:T(1,128)S(1)}, f32[1,4096]{1,0:T(1,128)S(1)}, u32[]{:S(2)}, u32[]{:S(2)}) collective-permute-start(f32[1,4096]{1,0:T(1,128)S(1)} %add.80), channel_id=1, source_target_pairs={{0,32},{16,48},{32,0},{48,16},{64,96},{80,112},{96,64},{112,80},{1... | collective-permute-start | bytes 49160 | tf_op jit(solution)/shard_map/ppermute | solution.py:43
  97.5 4.7 %collective-permute-start.27 = (f32[16,1536]{1,0:T(8,128)S(1)}, f32[16,1536]{1,0:T(8,128)S(1)}, u32[]{:S(2)}, u32[]{:S(2)}) collective-permute-start(f32[16,1536]{1,0:T(8,128)S(1)} %get-tuple-element.90), channel_id=1, source_target_pairs={{0,48},{16,0},{32,16},{48,32},{64,112},{80,64},{96,80},{112,96},{1... | collective-permute-start | bytes 294920 | tf_op jit(solution)/shard_map/ppermute | solution.py:43
